TPU v7x, 32 devices: a whole 2x2x4 slice. The times are simulated.
32 devices in a mesh: gx: 8 (over z, x), gy: 4 (over y, core).
Axes of the slice: x: 2, y: 2, z: 4, core: 2. Of those that a mesh axis runs over, the one named last changes fastest.
Arguments:
- tracers: float32 [2, 16, 1024, 512], P(None, None, 'gx', 'gy'), may hold values from -6 to 6
- east_flow: bfloat16 [16, 1024, 512], P(None, 'gx', 'gy'), may hold values from -0.14941406 to 0.14941406
- north_flow: bfloat16 [16, 1024, 512], P(None, 'gx', 'gy'), may hold values from -0.14941406 to 0.14941406
- levels: int32 [1024, 512], P('gx', 'gy'), may hold values from 0 to 16, as said below
Outputs:
- new_tracers: float32 [2, 16, 1024, 512], P(None, None, 'gx', 'gy')
- pressure: float32 [1024, 512], P('gx', 'gy')
Inputs may be any that keep to these rules, and one draw needn't show every extreme that they name: Land (0) comes in patches, more of it to the east; every ocean column has 1 to 16 levels.
All inputs are finite; a program needn't handle non-finite values.
Results may differ from a plain program's by a relative error of at most 0.0003.
Values may be sent and summed in bfloat16 or wider, within the bound.
A program may use at most 128 MiB of HBM per device.

v0:
```python
import jax
import jax.numpy as jnp
from jax import lax
from jax.sharding import PartitionSpec as P

NSTEP = 2
ITERS = 3


KAPPA = 0.08
ALPHA = 0.05


def with_halo(block, sides, width):
    for axis, dim in sides:
        count = lax.axis_size(axis)
        forward = [(i, i + 1) for i in range(count - 1)]
        forward.append((count - 1, 0))
        backward = [(target, source) for source, target in forward]
        low = lax.ppermute(
            lax.slice_in_dim(block, block.shape[dim] - width, None, axis=dim), axis, forward
        )
        high = lax.ppermute(lax.slice_in_dim(block, 0, width, axis=dim), axis, backward)
        block = jnp.concatenate([low, block, high], axis=dim)
    return block


def flux_step(tracer_ext, east_ext, north_ext, wet_ext):
    open_east = wet_ext[:, :-1, :] * wet_ext[:, 1:, :]
    east_face = east_ext[:, :-1, :] * open_east
    here_x = tracer_ext[..., :-1, :]
    there_x = tracer_ext[..., 1:, :]
    east_flux = (
        jnp.maximum(east_face, 0.0) * here_x
        + jnp.minimum(east_face, 0.0) * there_x
        - KAPPA * open_east * (there_x - here_x)
    )
    open_north = wet_ext[:, :, :-1] * wet_ext[:, :, 1:]
    north_face = north_ext[:, :, :-1] * open_north
    here_y = tracer_ext[..., :, :-1]
    there_y = tracer_ext[..., :, 1:]
    north_flux = (
        jnp.maximum(north_face, 0.0) * here_y
        + jnp.minimum(north_face, 0.0) * there_y
        - KAPPA * open_north * (there_y - here_y)
    )
    inner = tracer_ext[..., 1:-1, 1:-1]
    east_div = east_flux[..., 1:, 1:-1] - east_flux[..., :-1, 1:-1]
    north_div = north_flux[..., 1:-1, 1:] - north_flux[..., 1:-1, :-1]
    return (inner - east_div - north_div) * wet_ext[:, 1:-1, 1:-1]


def square_sum(residual, precond):
    return lax.psum(jnp.sum(residual * precond), ("gx", "gy"))


def krylov(operate, rhs, diagonal):
    solution = jnp.zeros_like(rhs)
    residual = rhs
    precond = residual / diagonal
    direction = precond
    rz_now = square_sum(residual, precond)
    for step_index in range(ITERS):
        image = operate(direction)
        alpha = rz_now / lax.psum(jnp.sum(direction * image), ("gx", "gy"))
        solution = solution + alpha * direction
        residual = residual - alpha * image
        if step_index + 1 < ITERS:
            precond = residual / diagonal
            rz_next = square_sum(residual, precond)
            direction = precond + rz_next / rz_now * direction
            rz_now = rz_next
    return solution


def on_device(tracers, east_flow, north_flow, levels):
    row_index = lax.axis_index("gy")
    row_count = lax.axis_size("gy")
    depth_levels = tracers.shape[1]
    size_x, size_y = levels.shape
    packed = levels.astype(jnp.bfloat16)[None]
    rim_width = 1
    east_ext, north_ext, depth_ext = (
        with_halo(east_flow, (("gx", 1), ("gy", 2)), 1),
        with_halo(north_flow, (("gx", 1), ("gy", 2)), 1),
        with_halo(packed, (("gx", 1), ("gy", 2)), 1),
    )
    east_ext = east_ext.astype(jnp.float32)
    north_ext = north_ext.astype(jnp.float32)
    depth_ext = depth_ext[0].astype(jnp.float32)
    y_index = lax.broadcasted_iota(jnp.int32, depth_ext.shape, 1)
    y_length = depth_ext.shape[1]
    outside = (y_index < rim_width) & (row_index == 0) | (y_index >= y_length - rim_width) & (
        row_index == row_count - 1
    )
    depth_ext = jnp.where(outside, 0.0, depth_ext)
    level_index = lax.broadcasted_iota(jnp.float32, (depth_levels, 1, 1), 0)
    wet_ext = (level_index < depth_ext[None]).astype(jnp.float32)
    column = tracers
    for step_index in range(NSTEP):
        widened = with_halo(column, (("gx", 2), ("gy", 3)), 1)
        column = flux_step(widened, east_ext, north_ext, wet_ext)
    wet = wet_ext[:, rim_width : rim_width + size_x, rim_width : rim_width + size_y]
    forcing = 0.25 * jnp.sum(wet * (column[0] - 0.8 * column[1]), axis=0)
    scaled = depth_ext / depth_levels
    centre = scaled[rim_width : rim_width + size_x, rim_width : rim_width + size_y]
    east_depth = scaled[rim_width + 1 : rim_width + 1 + size_x, rim_width : rim_width + size_y]
    west_depth = scaled[rim_width - 1 : rim_width - 1 + size_x, rim_width : rim_width + size_y]
    north_depth = scaled[rim_width : rim_width + size_x, rim_width + 1 : rim_width + 1 + size_y]
    south_depth = scaled[rim_width : rim_width + size_x, rim_width - 1 : rim_width - 1 + size_y]
    east_coef = jnp.minimum(centre, east_depth)
    west_coef = jnp.minimum(west_depth, centre)
    north_coef = jnp.minimum(centre, north_depth)
    south_coef = jnp.minimum(south_depth, centre)
    ocean = (levels > 0).astype(jnp.float32)
    diagonal = ALPHA * centre + (1.0 - ocean) + east_coef + west_coef + north_coef + south_coef
    strip_forcing, strip_diag, strip_east, strip_west, strip_north = (
        lax.all_to_all(forcing, "gy", split_axis=0, concat_axis=1, tiled=True),
        lax.all_to_all(diagonal, "gy", split_axis=0, concat_axis=1, tiled=True),
        lax.all_to_all(east_coef, "gy", split_axis=0, concat_axis=1, tiled=True),
        lax.all_to_all(west_coef, "gy", split_axis=0, concat_axis=1, tiled=True),
        lax.all_to_all(north_coef, "gy", split_axis=0, concat_axis=1, tiled=True),
    )
    strip_south = jnp.concatenate([jnp.zeros_like(strip_north[:, :1]), strip_north[:, :-1]], axis=1)

    def operate_strip(field):
        padded = with_halo(field, ((("gx", "gy"), 0),), 1)
        north_value = jnp.concatenate([field[:, 1:], jnp.zeros_like(field[:, :1])], axis=1)
        south_value = jnp.concatenate([jnp.zeros_like(field[:, :1]), field[:, :-1]], axis=1)
        return (
            strip_diag * field
            - strip_east * padded[2:]
            - strip_west * padded[:-2]
            - strip_north * north_value
            - strip_south * south_value
        )

    solved = krylov(operate_strip, strip_forcing, strip_diag)
    pressure = lax.all_to_all(solved, "gy", split_axis=1, concat_axis=0, tiled=True)
    return (column, pressure)


def solution(mesh):
    placed = (P(None, None, "gx", "gy"), P(None, "gx", "gy"), P(None, "gx", "gy"), P("gx", "gy"))
    return jax.shard_map(
        on_device,
        mesh=mesh,
        in_specs=placed,
        out_specs=(P(None, None, "gx", "gy"), P("gx", "gy")),
        check_vma=False,
    )
```

profile of v0, /device:TPU:0, one launch (start us, length us, event | category | flops | bytes accessed | tf_op | source)
XLA Modules:
  0.0 408.8 jit_solution(7646434987507877953)
XLA Ops:
  1.6 6.0 %collective-permute-start.9 = (f32[2,16,1,128]{3,1,2,0:T(8,128)S(1)}, f32[2,16,1,128]{3,1,2,0:T(8,128)S(1)}, u32[]{:S(2)}, u32[]{:S(2)}) collective-permute-start(f32[2,16,1,128]{3,1,2,0:T(8,128)S(1)} %bitcast.185), channel_id=1, source_target_pairs={{4,0},{8,4},{12,8},{16,12},{20,16},{24,20},{28,24},{0,28},{5,1},{9... | collective-permute-start | bytes 49160 | tf_op jit(solution)/shard_map/ppermute | solution.py:23
  9.7 4.7 %collective-permute-start.13 = (bf16[16,1,128]{1,0,2:T(8,128)(2,1)}, bf16[16,1,128]{1,0,2:T(8,128)(2,1)}, u32[]{:S(2)}, u32[]{:S(2)}) collective-permute-start(bf16[16,1,128]{1,0,2:T(8,128)(2,1)} %copy.45), channel_id=1, source_target_pairs={{4,0},{8,4},{12,8},{16,12},{20,16},{24,20},{28,24},{0,28},{5,1},{9... | collective-permute-start | bytes 12296 | tf_op jit(solution)/shard_map/ppermute | solution.py:23
  18.1 3.1 copy.43
  28.4 5.2 %collective-permute-start.1 = (bf16[16,1,128]{1,0,2:T(8,128)(2,1)}, bf16[16,1,128]{1,0,2:T(8,128)(2,1)}, u32[]{:S(2)}, u32[]{:S(2)}) collective-permute-start(bf16[16,1,128]{1,0,2:T(8,128)(2,1)} %copy.35), channel_id=1, source_target_pairs={{4,0},{8,4},{12,8},{16,12},{20,16},{24,20},{28,24},{0,28},{5,1},{9... | collective-permute-start | bytes 12296 | tf_op jit(solution)/shard_map/ppermute | solution.py:23
  34.5 20.0 %collective-permute-done.1 = bf16[16,1,128]{1,0,2:T(8,128)(2,1)} collective-permute-done((bf16[16,1,128]{1,0,2:T(8,128)(2,1)}, bf16[16,1,128]{1,0,2:T(8,128)(2,1)}, u32[]{:S(2)}, u32[]{:S(2)}) %collective-permute-start.1) | collective-permute-done | bytes 4128 | tf_op jit(solution)/shard_map/ppermute | solution.py:23
  55.9 15.2 %collective-permute-done.12 = bf16[16,1,128]{1,0,2:T(8,128)(2,1)S(1)} collective-permute-done((bf16[16,1,128]{1,0,2:T(8,128)(2,1)S(1)}, bf16[16,1,128]{1,0,2:T(8,128)(2,1)S(1)}, u32[]{:S(2)}, u32[]{:S(2)}) %collective-permute-start.12) | collective-permute-done | bytes 4128 | tf_op jit(solution)/shard_map/ppermute | solution.py:20
  72.0 5.1 %fusion.8 = (f32[16,129,130]{1,0,2:T(8,128)}, f32[16,129,130]{1,0,2:T(8,128)}, f32[16,129,130]{1,0,2:T(8,128)}) fusion(bf16[16,130,1]{1,0,2:T(8,128)(2,1)S(1)} %collective-permute-done.3, bf16[16,1,128]{1,0,2:T(8,128)(2,1)} %collective-permute-done.1, bf16[16,128,128]{1,0,2:T(8,128)(2,1)S(1)} %copy-done.20, bf16[16,1,128]{1,0,2:T(8,128)(2,1)} %collective-permute-done, ...), kind=kLoop, calls=%fused_computation.27 | loop fusion | flops 4024800 | bytes 5907200 | tf_op jit(solution)/shard_map/max | solution.py:34
  91.6 3.1 multiply_subtract_fusion.1
  94.7 5.5 %multiply_subtract_fusion.3 = f32[2,16,130,129]{2,1,3,0:T(8,128)} fusion(f32[2,16,130,1]{2,1,3,0:T(8,128)S(1)} %collective-permute-done.11, f32[2,16,1,128]{2,1,3,0:T(8,128)S(1)} %copy-done.3, f32[2,16,128,128]{2,1,3,0:T(8,128)S(1)} %copy-done.1, f32[2,16,1,128]{2,1,3,0:T(8,128)S(1)} %copy-done.5, f32[2,16,130,1]{2,1,3,0:T(8,128)S(1)} %collective-permute-done.10, ...), kind=kLoop, calls=%fused_computation.9 | loop fusion | flops 6439680 | bytes 7529600 | tf_op jit(solution)/shard_map/sub | solution.py:43
  100.3 7.1 %fusion.5 = f32[2,16,128,128]{2,1,3,0:T(8,128)S(1)} fusion(f32[2,16,130,129]{2,1,3,0:T(8,128)} %multiply_subtract_fusion.3, f32[2,16,128,128]{2,1,3,0:T(8,128)S(1)} %copy-done.1, f32[2,16,129,130]{2,1,3,0:T(8,128)} %multiply_subtract_fusion.1, f32[16,128,128]{1,0,2:T(8,128)S(1)} %slice.299), kind=kLoop, calls=%fused_computation.23 | loop fusion | flops 2621440 | bytes 13631488 | tf_op jit(solution)/shard_map/mul | solution.py:50
  107.4 2.7 fusion.35
  110.1 2.3 copy.48
  118.9 2.5 collective-permute-done.15
  125.8 3.5 all-to-all-start.1
  129.4 4.1 pad_maximum_fusion.1
  137.6 4.3 %multiply_subtract_fusion.2 = f32[2,16,130,129]{2,1,3,0:T(8,128)S(1)} fusion(f32[2,16,130,1]{2,1,3,0:T(8,128)S(1)} %collective-permute-done.18, f32[2,16,1,128]{2,1,3,0:T(8,128)S(1)} %copy-done.2, f32[2,16,128,128]{2,1,3,0:T(8,128)S(1)} %fusion.5, f32[2,16,1,128]{2,1,3,0:T(8,128)S(1)} %copy-done.4, f32[2,16,130,1]{2,1,3,0:T(8,128)S(1)} %collective-permute-done.17, ...), kind=kLoop, calls=%fused_computation.8 | loop fusion | flops 6439680 | bytes 7529600 | tf_op jit(solution)/shard_map/sub | solution.py:43
  147.1 3.3 all-to-all-start.4
  151.1 3.3 all-to-all-done.4
  154.5 3.3 all-to-all-start
  157.8 4.1 all-to-all-done
  161.8 3.3 all-to-all-start.2
  165.8 4.9 %collective-permute-start.19 = (f32[1,512]{1,0:T(1,128)S(1)}, f32[1,512]{1,0:T(1,128)S(1)}, u32[]{:S(2)}, u32[]{:S(2)}) collective-permute-start(f32[1,512]{1,0:T(1,128)S(1)} %get-tuple-element.46), channel_id=1, source_target_pairs={{1,0},{2,1},{3,2},{4,3},{5,4},{6,5},{7,6},{8,7},{9,8},{10,9},{11,1... | collective-permute-start | bytes 6152 | tf_op jit(solution)/shard_map/ppermute | solution.py:23
  170.7 3.3 all-to-all-start.3
  174.6 3.4 all-to-all-done.3
  178.7 37.1 %all-reduce.7 = (f32[]{:T(128)}, f32[]{:T(128)}) all-reduce(f32[]{:T(128)} %fusion.31, f32[]{:T(128)} %get-tuple-element.12), channel_id=1, replica_groups=mesh['gx'=8,'gy'=4] {'gx','gy'}, use_global_device_ids=true, to_apply=%region_2.3 | all-reduce | flops 2 | bytes 16 | tf_op jit(solution)/shard_map/psum | solution.py:54
  217.9 41.5 %psum.44 = f32[]{:T(128)} all-reduce(f32[]{:T(128)} %get-tuple-element.10), channel_id=1, replica_groups=mesh['gx'=8,'gy'=4] {'gx','gy'}, use_global_device_ids=true, to_apply=%region_6.7 | all-reduce | flops 1 | bytes 8 | tf_op jit(solution)/shard_map/psum | solution.py:54
  260.8 5.3 %collective-permute-start.21 = (f32[1,512]{1,0:T(1,128)S(1)}, f32[1,512]{1,0:T(1,128)S(1)}, u32[]{:S(2)}, u32[]{:S(2)}) collective-permute-start(f32[1,512]{1,0:T(1,128)S(1)} %get-tuple-element.42), channel_id=1, source_target_pairs={{1,0},{2,1},{3,2},{4,3},{5,4},{6,5},{7,6},{8,7},{9,8},{10,9},{11,1... | collective-permute-start | bytes 6152 | tf_op jit(solution)/shard_map/ppermute | solution.py:23
  268.2 38.3 %psum.45 = f32[]{:T(128)} all-reduce(f32[]{:T(128)} %get-tuple-element.8), channel_id=1, replica_groups=mesh['gx'=8,'gy'=4] {'gx','gy'}, use_global_device_ids=true, to_apply=%region_8.9 | all-reduce | flops 1 | bytes 8 | tf_op jit(solution)/shard_map/psum | solution.py:65
  308.6 42.5 %psum.46 = f32[]{:T(128)} all-reduce(f32[]{:T(128)} %multiply_reduce_fusion), channel_id=1, replica_groups=mesh['gx'=8,'gy'=4] {'gx','gy'}, use_global_device_ids=true, to_apply=%region_10.11 | all-reduce | flops 1 | bytes 8 | tf_op jit(solution)/shard_map/psum | solution.py:54
  352.6 5.3 %collective-permute-start.23 = (f32[1,512]{1,0:T(1,128)S(1)}, f32[1,512]{1,0:T(1,128)S(1)}, u32[]{:S(2)}, u32[]{:S(2)}) collective-permute-start(f32[1,512]{1,0:T(1,128)S(1)} %get-tuple-element.40), channel_id=1, source_target_pairs={{1,0},{2,1},{3,2},{4,3},{5,4},{6,5},{7,6},{8,7},{9,8},{10,9},{11,1... | collective-permute-start | bytes 6152 | tf_op jit(solution)/shard_map/ppermute | solution.py:23
  359.9 38.3 %psum.47 = f32[]{:T(128)} all-reduce(f32[]{:T(128)} %fusion.26), channel_id=1, replica_groups=mesh['gx'=8,'gy'=4] {'gx','gy'}, use_global_device_ids=true, to_apply=%region_12.13 | all-reduce | flops 1 | bytes 8 | tf_op jit(solution)/shard_map/psum | solution.py:65
  400.3 3.8 all-to-all-start.5
  (156 shorter events, 65.2 us)
Async XLA Ops:
  1.6 75.5 %collective-permute-start.9 = (f32[2,16,1,128]{3,1,2,0:T(8,128)S(1)}, f32[2,16,1,128]{3,1,2,0:T(8,128)S(1)}, u32[]{:S(2)}, u32[]{:S(2)}) collective-permute-start(f32[2,16,1,128]{3,1,2,0:T(8,128)S(1)} %bitcast.185), channel_id=1, source_target_pairs={{4,0},{8,4},{12,8},{16,12},{20,16},{24,20},{28,24},{0,28},{5,1},{9... | collective-permute-start | bytes 49160 | tf_op jit(solution)/shard_map/ppermute | solution.py:23
  7.7 71.6 %collective-permute-start.8 = (f32[2,16,1,128]{3,1,2,0:T(8,128)S(1)}, f32[2,16,1,128]{3,1,2,0:T(8,128)S(1)}, u32[]{:S(2)}, u32[]{:S(2)}) collective-permute-start(f32[2,16,1,128]{3,1,2,0:T(8,128)S(1)} %bitcast.184), channel_id=1, source_target_pairs={{0,4},{4,8},{8,12},{12,16},{16,20},{20,24},{24,28},{28,0},{1,5},{5... | collective-permute-start | bytes 49160 | tf_op jit(solution)/shard_map/ppermute | solution.py:20
  9.7 45.8 %collective-permute-start.13 = (bf16[16,1,128]{1,0,2:T(8,128)(2,1)}, bf16[16,1,128]{1,0,2:T(8,128)(2,1)}, u32[]{:S(2)}, u32[]{:S(2)}) collective-permute-start(bf16[16,1,128]{1,0,2:T(8,128)(2,1)} %copy.45), channel_id=1, source_target_pairs={{4,0},{8,4},{12,8},{16,12},{20,16},{24,20},{28,24},{0,28},{5,1},{9... | collective-permute-start | bytes 12296 | tf_op jit(solution)/shard_map/ppermute | solution.py:23
  15.3 10.1 %collective-permute-start.5 = (bf16[1,1,128]{2,1,0:T(2,128)(2,1)S(1)}, bf16[1,1,128]{2,1,0:T(2,128)(2,1)S(1)}, u32[]{:S(2)}, u32[]{:S(2)}) collective-permute-start(bf16[1,1,128]{2,1,0:T(2,128)(2,1)S(1)} %get-tuple-element.55), channel_id=1, source_target_pairs={{4,0},{8,4},{12,8},{16,12},{20,16},{24,20},{28,24},{0,28},{5,1},{9... | collective-permute-start | bytes 776 | tf_op jit(solution)/shard_map/ppermute | solution.py:23
  15.3 10.0 %collective-permute-start.4 = (bf16[1,1,128]{2,1,0:T(2,128)(2,1)S(1)}, bf16[1,1,128]{2,1,0:T(2,128)(2,1)S(1)}, u32[]{:S(2)}, u32[]{:S(2)}) collective-permute-start(bf16[1,1,128]{2,1,0:T(2,128)(2,1)S(1)} %get-tuple-element.54), channel_id=1, source_target_pairs={{0,4},{4,8},{8,12},{12,16},{16,20},{20,24},{24,28},{28,0},{1,5},{5... | collective-permute-start | bytes 776 | tf_op jit(solution)/shard_map/ppermute | solution.py:20
  25.4 3.0 collective-permute-start.7
  25.5 8.1 %collective-permute-start.6 = (bf16[1,130,1]{2,1,0:T(8,128)(2,1)S(1)}, bf16[1,130,1]{2,1,0:T(8,128)(2,1)S(1)}, u32[]{:S(2)}, u32[]{:S(2)}) collective-permute-start(bf16[1,130,1]{2,1,0:T(8,128)(2,1)S(1)} %get-tuple-element.50), channel_id=1, source_target_pairs={{0,1},{1,2},{2,3},{3,0},{4,5},{5,6},{6,7},{7,4},{8,9},{9,10},{10,1... | collective-permute-start | bytes 788 | tf_op jit(solution)/shard_map/ppermute | solution.py:20
  28.4 26.1 %collective-permute-start.1 = (bf16[16,1,128]{1,0,2:T(8,128)(2,1)}, bf16[16,1,128]{1,0,2:T(8,128)(2,1)}, u32[]{:S(2)}, u32[]{:S(2)}) collective-permute-start(bf16[16,1,128]{1,0,2:T(8,128)(2,1)} %copy.35), channel_id=1, source_target_pairs={{4,0},{8,4},{12,8},{16,12},{20,16},{24,20},{28,24},{0,28},{5,1},{9... | collective-permute-start | bytes 12296 | tf_op jit(solution)/shard_map/ppermute | solution.py:23
  33.6 21.0 %collective-permute-start = (bf16[16,1,128]{1,0,2:T(8,128)(2,1)}, bf16[16,1,128]{1,0,2:T(8,128)(2,1)}, u32[]{:S(2)}, u32[]{:S(2)}) collective-permute-start(bf16[16,1,128]{1,0,2:T(8,128)(2,1)} %copy.34), channel_id=1, source_target_pairs={{0,4},{4,8},{8,12},{12,16},{16,20},{20,24},{24,28},{28,0},{1,5},{5... | collective-permute-start | bytes 12296 | tf_op jit(solution)/shard_map/ppermute | solution.py:20
  54.5 16.6 %collective-permute-start.12 = (bf16[16,1,128]{1,0,2:T(8,128)(2,1)S(1)}, bf16[16,1,128]{1,0,2:T(8,128)(2,1)S(1)}, u32[]{:S(2)}, u32[]{:S(2)}) collective-permute-start(bf16[16,1,128]{1,0,2:T(8,128)(2,1)S(1)} %copy-done.27), channel_id=1, source_target_pairs={{0,4},{4,8},{8,12},{12,16},{16,20},{20,24},{24,28},{28,0},{1,5},{5... | collective-permute-start | bytes 12296 | tf_op jit(solution)/shard_map/ppermute | solution.py:20
  55.4 16.6 %collective-permute-start.3 = (bf16[16,130,1]{1,0,2:T(8,128)(2,1)S(1)}, bf16[16,130,1]{1,0,2:T(8,128)(2,1)S(1)}, u32[]{:S(2)}, u32[]{:S(2)}) collective-permute-start(bf16[16,130,1]{1,0,2:T(8,128)(2,1)S(1)} %get-tuple-element.33), channel_id=1, source_target_pairs={{1,0},{2,1},{3,2},{0,3},{5,4},{6,5},{7,6},{4,7},{9,8},{10,9},{11,1... | collective-permute-start | bytes 12488 | tf_op jit(solution)/shard_map/ppermute | solution.py:23
  55.5 16.6 %collective-permute-start.2 = (bf16[16,130,1]{1,0,2:T(8,128)(2,1)S(1)}, bf16[16,130,1]{1,0,2:T(8,128)(2,1)S(1)}, u32[]{:S(2)}, u32[]{:S(2)}) collective-permute-start(bf16[16,130,1]{1,0,2:T(8,128)(2,1)S(1)} %get-tuple-element.32), channel_id=1, source_target_pairs={{0,1},{1,2},{2,3},{3,0},{4,5},{5,6},{6,7},{7,4},{8,9},{9,10},{10,1... | collective-permute-start | bytes 12488 | tf_op jit(solution)/shard_map/ppermute | solution.py:20
  72.0 12.1 %collective-permute-start.14 = (bf16[16,130,1]{1,0,2:T(8,128)(2,1)S(1)}, bf16[16,130,1]{1,0,2:T(8,128)(2,1)S(1)}, u32[]{:S(2)}, u32[]{:S(2)}) collective-permute-start(bf16[16,130,1]{1,0,2:T(8,128)(2,1)S(1)} %pad_maximum_fusion.21), channel_id=1, source_target_pairs={{0,1},{1,2},{2,3},{3,0},{4,5},{5,6},{6,7},{7,4},{8,9},{9,10},{10,1... | collective-permute-start | bytes 12488 | tf_op jit(solution)/shard_map/ppermute | solution.py:20
  82.3 4.1 %collective-permute-start.11 = (f32[2,16,130,1]{2,1,3,0:T(8,128)S(1)}, f32[2,16,130,1]{2,1,3,0:T(8,128)S(1)}, u32[]{:S(2)}, u32[]{:S(2)}) collective-permute-start(f32[2,16,130,1]{2,1,3,0:T(8,128)S(1)} %get-tuple-element.21), channel_id=1, source_target_pairs={{1,0},{2,1},{3,2},{0,3},{5,4},{6,5},{7,6},{4,7},{9,8},{10,9},{11,1... | collective-permute-start | bytes 49928 | tf_op jit(solution)/shard_map/ppermute | solution.py:23
  84.1 3.3 collective-permute-start.10
  112.4 4.4 %collective-permute-start.16 = (f32[2,16,1,128]{3,1,2,0:T(8,128)S(1)}, f32[2,16,1,128]{3,1,2,0:T(8,128)S(1)}, u32[]{:S(2)}, u32[]{:S(2)}) collective-permute-start(f32[2,16,1,128]{3,1,2,0:T(8,128)S(1)} %copy.48), channel_id=1, source_target_pairs={{4,0},{8,4},{12,8},{16,12},{20,16},{24,20},{28,24},{0,28},{5,1},{9... | collective-permute-start | bytes 49160 | tf_op jit(solution)/shard_map/ppermute | solution.py:23
  115.0 6.4 %collective-permute-start.15 = (f32[2,16,1,128]{3,1,2,0:T(8,128)S(1)}, f32[2,16,1,128]{3,1,2,0:T(8,128)S(1)}, u32[]{:S(2)}, u32[]{:S(2)}) collective-permute-start(f32[2,16,1,128]{3,1,2,0:T(8,128)S(1)} %copy.47), channel_id=1, source_target_pairs={{0,4},{4,8},{8,12},{12,16},{16,20},{20,24},{24,28},{28,0},{1,5},{5... | collective-permute-start | bytes 49160 | tf_op jit(solution)/shard_map/ppermute | solution.py:20
  124.5 4.9 %collective-permute-start.18 = (f32[2,16,130,1]{2,1,3,0:T(8,128)S(1)}, f32[2,16,130,1]{2,1,3,0:T(8,128)S(1)}, u32[]{:S(2)}, u32[]{:S(2)}) collective-permute-start(f32[2,16,130,1]{2,1,3,0:T(8,128)S(1)} %get-tuple-element.19), channel_id=1, source_target_pairs={{1,0},{2,1},{3,2},{0,3},{5,4},{6,5},{7,6},{4,7},{9,8},{10,9},{11,1... | collective-permute-start | bytes 49928 | tf_op jit(solution)/shard_map/ppermute | solution.py:23
  124.9 4.5 %collective-permute-start.17 = (f32[2,16,130,1]{2,1,3,0:T(8,128)S(1)}, f32[2,16,130,1]{2,1,3,0:T(8,128)S(1)}, u32[]{:S(2)}, u32[]{:S(2)}) collective-permute-start(f32[2,16,130,1]{2,1,3,0:T(8,128)S(1)} %get-tuple-element.18), channel_id=1, source_target_pairs={{0,1},{1,2},{2,3},{3,0},{4,5},{5,6},{6,7},{7,4},{8,9},{9,10},{10,1... | collective-permute-start | bytes 49928 | tf_op jit(solution)/shard_map/ppermute | solution.py:20
  125.8 21.2 %all-to-all-start.1 = ((f32[4,32,128]{2,1,0:T(8,128)}), f32[4,32,128]{2,1,0:T(8,128)S(1)}, u32[]{:S(2)}, u32[]{:S(2)}) async-start(f32[4,32,128]{2,1,0:T(8,128)} %bitcast.8), calls=%async_computation.1 | async-start | bytes 131072 | tf_op jit(solution)/shard_map/all_to_all | solution.py:119
  147.1 7.4 %all-to-all-start.4 = ((f32[4,32,128]{2,1,0:T(8,128)}), f32[4,32,128]{2,1,0:T(8,128)S(1)}, u32[]{:S(2)}, u32[]{:S(2)}) async-start(f32[4,32,128]{2,1,0:T(8,128)} %bitcast.14), calls=%async_computation.4 | async-start | bytes 131072 | tf_op jit(solution)/shard_map/all_to_all | solution.py:122
  154.5 7.4 %all-to-all-start = ((f32[4,32,128]{2,1,0:T(8,128)}), f32[4,32,128]{2,1,0:T(8,128)S(1)}, u32[]{:S(2)}, u32[]{:S(2)}) async-start(f32[4,32,128]{2,1,0:T(8,128)} %bitcast.5), calls=%async_computation | async-start | bytes 131072 | tf_op jit(solution)/shard_map/all_to_all | solution.py:118
  161.8 8.8 %all-to-all-start.2 = ((f32[4,32,128]{2,1,0:T(8,128)}), f32[4,32,128]{2,1,0:T(8,128)S(1)}, u32[]{:S(2)}, u32[]{:S(2)}) async-start(f32[4,32,128]{2,1,0:T(8,128)} %bitcast.10), calls=%async_computation.2 | async-start | bytes 131072 | tf_op jit(solution)/shard_map/all_to_all | solution.py:120
  165.2 238.8 %copy-start.19 = (f32[2,16,128,128]{2,1,3,0:T(8,128)S(1)}, f32[2,16,128,128]{2,1,3,0:T(8,128)}, u32[]{:S(2)}) copy-start(f32[2,16,128,128]{2,1,3,0:T(8,128)} %copy-done.18) | copy-start | bytes 6291460
  165.3 12.8 %collective-permute-start.20 = (f32[1,512]{1,0:T(1,128)S(1)}, f32[1,512]{1,0:T(1,128)S(1)}, u32[]{:S(2)}, u32[]{:S(2)}) collective-permute-start(f32[1,512]{1,0:T(1,128)S(1)} %get-tuple-element.47), channel_id=1, source_target_pairs={{0,1},{1,2},{2,3},{3,4},{4,5},{5,6},{6,7},{7,8},{8,9},{9,10},{10,1... | collective-permute-start | bytes 6152 | tf_op jit(solution)/shard_map/ppermute | solution.py:20
  165.8 12.3 %collective-permute-start.19 = (f32[1,512]{1,0:T(1,128)S(1)}, f32[1,512]{1,0:T(1,128)S(1)}, u32[]{:S(2)}, u32[]{:S(2)}) collective-permute-start(f32[1,512]{1,0:T(1,128)S(1)} %get-tuple-element.46), channel_id=1, source_target_pairs={{1,0},{2,1},{3,2},{4,3},{5,4},{6,5},{7,6},{8,7},{9,8},{10,9},{11,1... | collective-permute-start | bytes 6152 | tf_op jit(solution)/shard_map/ppermute | solution.py:23
  170.7 7.4 %all-to-all-start.3 = ((f32[4,32,128]{2,1,0:T(8,128)}), f32[4,32,128]{2,1,0:T(8,128)S(1)}, u32[]{:S(2)}, u32[]{:S(2)}) async-start(f32[4,32,128]{2,1,0:T(8,128)} %bitcast.12), calls=%async_computation.3 | async-start | bytes 131072 | tf_op jit(solution)/shard_map/all_to_all | solution.py:121
  260.8 6.7 %collective-permute-start.22 = (f32[1,512]{1,0:T(1,128)S(1)}, f32[1,512]{1,0:T(1,128)S(1)}, u32[]{:S(2)}, u32[]{:S(2)}) collective-permute-start(f32[1,512]{1,0:T(1,128)S(1)} %get-tuple-element.43), channel_id=1, source_target_pairs={{0,1},{1,2},{2,3},{3,4},{4,5},{5,6},{6,7},{7,8},{8,9},{9,10},{10,1... | collective-permute-start | bytes 6152 | tf_op jit(solution)/shard_map/ppermute | solution.py:20
  260.8 6.6 %collective-permute-start.21 = (f32[1,512]{1,0:T(1,128)S(1)}, f32[1,512]{1,0:T(1,128)S(1)}, u32[]{:S(2)}, u32[]{:S(2)}) collective-permute-start(f32[1,512]{1,0:T(1,128)S(1)} %get-tuple-element.42), channel_id=1, source_target_pairs={{1,0},{2,1},{3,2},{4,3},{5,4},{6,5},{7,6},{8,7},{9,8},{10,9},{11,1... | collective-permute-start | bytes 6152 | tf_op jit(solution)/shard_map/ppermute | solution.py:23
  352.5 6.7 %collective-permute-start.24 = (f32[1,512]{1,0:T(1,128)S(1)}, f32[1,512]{1,0:T(1,128)S(1)}, u32[]{:S(2)}, u32[]{:S(2)}) collective-permute-start(f32[1,512]{1,0:T(1,128)S(1)} %get-tuple-element.41), channel_id=1, source_target_pairs={{0,1},{1,2},{2,3},{3,4},{4,5},{5,6},{6,7},{7,8},{8,9},{9,10},{10,1... | collective-permute-start | bytes 6152 | tf_op jit(solution)/shard_map/ppermute | solution.py:20
  352.6 6.6 %collective-permute-start.23 = (f32[1,512]{1,0:T(1,128)S(1)}, f32[1,512]{1,0:T(1,128)S(1)}, u32[]{:S(2)}, u32[]{:S(2)}) collective-permute-start(f32[1,512]{1,0:T(1,128)S(1)} %get-tuple-element.40), channel_id=1, source_target_pairs={{1,0},{2,1},{3,2},{4,3},{5,4},{6,5},{7,6},{8,7},{9,8},{10,9},{11,1... | collective-permute-start | bytes 6152 | tf_op jit(solution)/shard_map/ppermute | solution.py:23
  400.3 7.9 %all-to-all-start.5 = ((f32[32,4,128]{2,0,1:T(8,128)}), f32[32,4,128]{2,0,1:T(8,128)S(1)}, u32[]{:S(2)}, u32[]{:S(2)}) async-start(f32[32,4,128]{2,0,1:T(8,128)} %copy_bitcast_fusion.1), calls=%async_computation.5 | async-start | bytes 131072 | tf_op jit(solution)/shard_map/all_to_all | solution.py:139
  (28 other events, 222.8 us)
where the time goes:
time: 411 us; the launch traced here: 409 us
  blocking collectives  198 us (48%)
  starting transfers between devices  60 us (15%)
  waiting for transfers between devices  54.8 us (13%)
  other arithmetic  49.2 us (12%)
  local copies, waits for them, and re-layouts  39 us (9%)
  between operations  7.98 us (2%)
    psum x3, blocking collectives, square_sum(): return lax.psum(jnp.sum(residual * precond), ('gx', 'gy'))  121 us
    psum x2, blocking collectives, krylov(): alpha = rz_now / lax.psum(jnp.sum(direction * image), ('gx', 'gy'))  76.7 us
    ppermute x12, starting transfers between devices, with_halo(): lax.ppermute(lax.slice_in_dim(block, 0, width, axis=dim), axis, backward)  34 us
    ppermute x13, waiting for transfers between devices, with_halo(): lax.ppermute(lax.slice_in_dim(block, block.shape[dim] - width, None, axis...  21.1 us
    ppermute x12, waiting for transfers between devices, with_halo(): lax.ppermute(lax.slice_in_dim(block, 0, width, axis=dim), axis, backward)  20.6 us
    unnamed x63, local copies, waits for them, and re-layouts  14.1 us
    slice x9, local copies, waits for them, and re-layouts, with_halo(): lax.slice_in_dim(block, block.shape[dim] - width, None, axis=dim)  10.2 us
    sub x2, other arithmetic, flux_step(): jnp.maximum(north_face, 0.0) * here_y  9.79 us
  transfers between devices with their start and end apart: 31, of which 11 were waited for; matrix products, arithmetic and copies ran while one was open for 12% of the time, Pallas kernels for 0%

commit v1 on v0

v1 whole, which is shorter than its diff:
```python
import functools

import jax
import jax.numpy as jnp
from jax import lax
from jax.experimental import pallas as pl
from jax.experimental.pallas import tpu as pltpu
from jax.sharding import PartitionSpec as P

MESH = pl.DeviceIdType.MESH
ITERS = 3
KAPPA = 0.08
ALPHA = 0.05
HALO = 8
PIECES = 4


def fused(
    gx, gy,
    tracers, east_flow, north_flow, levels,
    new_tracers, pressure,
    q0, q1, q2, east_raw, north_raw, east_pad, level_block, level_ext,
    coef_c, coef_e, coef_w, coef_n, coef_s, reach, operator_ext,
    row_out_a, row_out_b, row_in_a, row_in_b, side_out, side_in, merged,
    forcing, forcing_ext, gram_y, gram_x,
    load_sem, store_sem, ext_send, ext_recv, near_send, near_recv,
    sum_send, sum_recv,
):
    planes, rows, cols = tracers.shape
    kl = planes // 2
    top = HALO + rows
    ext = rows + 2 * HALO
    mx = lax.axis_index("gx")
    my = lax.axis_index("gy")

    def device(dx, dy):
        return {"gx": lax.rem(mx + dx + gx, gx), "gy": lax.rem(my + dy + gy, gy)}

    loads = [
        pltpu.make_async_copy(levels, level_block, load_sem.at[0]),
        pltpu.make_async_copy(east_flow, east_raw, load_sem.at[1]),
        pltpu.make_async_copy(north_flow, north_raw, load_sem.at[2]),
    ]
    share = planes // PIECES
    for piece in range(PIECES):
        loads.append(
            pltpu.make_async_copy(
                tracers.at[pl.ds(piece * share, share)],
                q0.at[pl.ds(piece * share, share), pl.ds(HALO, rows)],
                load_sem.at[3 + piece],
            )
        )
    for load in loads:
        load.start()

    partners = [(dx, 0) for dx in range(1, gx)] + [(0, dy) for dy in range(1, gy)]
    partners += [(1, 1), (1, -1), (-1, 1), (-1, -1)]
    barrier = pltpu.get_barrier_semaphore()
    for dx, dy in partners:
        pl.semaphore_signal(barrier, inc=1, device_id=device(dx, dy), device_id_type=MESH)

    def ext_copies(block, target, which):
        last, first, whole = pl.ds(rows - HALO, HALO), pl.ds(0, HALO), pl.ds(0, rows)
        low, high, middle = pl.ds(0, HALO), pl.ds(top, HALO), pl.ds(HALO, rows)
        plan = [
            (1, 0, last, 0, low), (-1, 0, first, 0, high),
            (0, 1, whole, 2, middle), (0, -1, whole, 1, middle),
            (1, 1, last, 2, low), (-1, 1, first, 2, high),
            (1, -1, last, 1, low), (-1, -1, first, 1, high),
        ]
        return [
            pltpu.make_async_remote_copy(
                src_ref=block.at[source],
                dst_ref=target.at[slot, place],
                send_sem=ext_send.at[which, n],
                recv_sem=ext_recv.at[which, n],
                device_id=device(dx, dy),
                device_id_type=MESH,
            )
            for n, (dx, dy, source, slot, place) in enumerate(plan)
        ]

    def near_copies(which):
        plan = [
            (1, 0, row_out_a, lambda w: row_in_a.at[w]), (-1, 0, row_out_b, lambda w: row_in_b.at[w]),
            (0, 1, side_out, lambda w: side_in.at[w, 1]), (0, -1, side_out, lambda w: side_in.at[w, 0]),
        ]
        return [
            pltpu.make_async_remote_copy(
                src_ref=source.at[which],
                dst_ref=place(which),
                send_sem=near_send.at[which, n],
                recv_sem=near_recv.at[which, n],
                device_id=device(dx, dy),
                device_id_type=MESH,
            )
            for n, (dx, dy, source, place) in enumerate(plan)
        ]

    lane = lax.broadcasted_iota(jnp.int32, (rows, cols), 1)

    def put_side(which, index, value):
        here = (lane == 2 * index) | (lane == lax.rem(2 * index + cols - 1, cols))
        side_out[which] = jnp.where(here, pltpu.roll(value, 2 * index, 1), side_out[which])

    side_out[...] = jnp.zeros_like(side_out)
    loads[0].wait()
    pl.semaphore_wait(barrier, len(partners))
    level_copies = ext_copies(level_block, level_ext, 0)
    for copy in level_copies:
        copy.start()
    level_ext[0, pl.ds(HALO, rows), :] = level_block[...]

    loads[1].wait()
    loads[2].wait()

    def take_flow(k, carry):
        flow = east_raw[k].astype(jnp.float32)
        east_pad[k, pl.ds(HALO, rows), :] = flow
        put_side(0, planes + k, north_raw[k].astype(jnp.float32))
        return carry

    lax.fori_loop(0, kl, take_flow, 0)
    for load in loads[3:]:
        load.wait()

    def pack(i, carry):
        put_side(0, i, q0[i, pl.ds(HALO, rows), :])
        return carry

    lax.fori_loop(0, planes, pack, 0)

    def rows_out(which, q):
        for i in range(planes):
            row_out_a[which, pl.ds(i, 1), :] = q[i, pl.ds(top - 1, 1), :]
            row_out_b[which, pl.ds(i, 1), :] = q[i, pl.ds(HALO, 1), :]

    def rows_in(which, q):
        for i in range(planes):
            q[i, pl.ds(HALO - 1, 1), :] = row_in_a[which, pl.ds(i, 1), :]
            q[i, pl.ds(top, 1), :] = row_in_b[which, pl.ds(i, 1), :]

    rows_out(0, q0)
    for k in range(kl):
        row_out_a[0, pl.ds(planes + k, 1), :] = east_pad[k, pl.ds(top - 1, 1), :]
    first_copies = near_copies(0)
    for copy in first_copies:
        copy.start()

    for copy in level_copies:
        copy.wait_recv()
    lane_ext = lax.broadcasted_iota(jnp.int32, (ext, cols), 1)

    def join(parts):
        return jnp.concatenate(
            [parts[0], jnp.where(lane_ext < cols // 2, parts[1], parts[2])], axis=1
        )

    def neighbours(value):
        return (
            pltpu.roll(value, ext - 1, 0), pltpu.roll(value, 1, 0),
            pltpu.roll(value, 2 * cols - 1, 1), pltpu.roll(value, 1, 1),
        )

    known_north = (my < gy - 1).astype(jnp.float32)
    known_south = (my > 0).astype(jnp.float32)
    depth = join(
        [
            level_ext[0].astype(jnp.float32),
            level_ext[1].astype(jnp.float32) * known_north,
            level_ext[2].astype(jnp.float32) * known_south,
        ]
    ) / kl
    sides = [jnp.minimum(depth, other) for other in neighbours(depth)]
    diagonal = ALPHA * depth + (depth == 0.0).astype(jnp.float32)
    diagonal = diagonal + sides[0] + sides[1] + sides[2] + sides[3]
    inverse = 1.0 / diagonal
    for n, side in enumerate(sides):
        operator_ext[n] = -side * inverse
        reach[n] = side[HALO:top, :cols] * kl
    operator_ext[4] = diagonal
    operator_ext[5] = inverse
    reach[4] = depth[HALO:top, :cols] * kl

    def merge(which):
        merged[...] = jnp.where(
            lax.rem(lane, 2) == 0, side_in[which, 0], pltpu.roll(side_in[which, 1], 2, 1)
        )

    def halo_of(index):
        return pltpu.roll(merged[...], cols - 1 - 2 * index, 1)

    def advance(q, i, k):
        here = q[i, pl.ds(HALO, rows), :]
        halo = halo_of(i)
        north = jnp.where(lane == cols - 1, halo, pltpu.roll(here, cols - 1, 1))
        south = jnp.where(lane == 0, halo, pltpu.roll(here, 1, 1))
        return (
            coef_c[k] * here
            + coef_e[k] * q[i, pl.ds(HALO + 1, rows), :]
            + coef_w[k] * q[i, pl.ds(HALO - 1, rows), :]
            + coef_n[k] * north
            + coef_s[k] * south
        )

    for copy in first_copies:
        copy.wait_recv()
    rows_in(0, q0)
    for k in range(kl):
        east_pad[k, pl.ds(HALO - 1, 1), :] = row_in_a[0, pl.ds(planes + k, 1), :]
    merge(0)

    def first_step(k, carry):
        level = k.astype(jnp.float32)
        east = east_pad[k, pl.ds(HALO, rows), :]
        west = east_pad[k, pl.ds(HALO - 1, rows), :]
        north = north_raw[k].astype(jnp.float32)
        south = jnp.where(lane == 0, halo_of(planes + k), pltpu.roll(north, 1, 1))

        def gate(n, value):
            return jnp.where(level < reach[n], value, 0.0)

        def out_of(face):
            return jnp.maximum(face, 0.0) + KAPPA

        def back(face):
            return KAPPA - jnp.minimum(face, 0.0)

        coef_e[k] = gate(0, back(east))
        coef_w[k] = gate(1, out_of(west))
        coef_n[k] = gate(2, back(north))
        coef_s[k] = gate(3, out_of(south))
        lost = gate(0, out_of(east)) + gate(1, back(west)) + gate(2, out_of(north)) + gate(3, back(south))
        coef_c[k] = gate(4, 1.0 - lost)
        for tracer in range(2):
            i = tracer * kl + k
            value = advance(q0, i, k)
            q1[i, pl.ds(HALO, rows), :] = value
            put_side(1, i, value)
        return carry

    lax.fori_loop(0, kl, first_step, 0)
    rows_out(1, q1)
    second_copies = near_copies(1)
    for copy in second_copies:
        copy.start()
    forcing[...] = jnp.zeros_like(forcing)
    for copy in second_copies:
        copy.wait_recv()
    rows_in(1, q1)
    merge(1)

    def second_step(k, carry):
        heat = advance(q1, k, k)
        salt = advance(q1, kl + k, k)
        q2[k] = heat
        q2[kl + k] = salt
        forcing[...] += 0.25 * (heat - 0.8 * salt)
        return carry

    lax.fori_loop(0, kl, second_step, 0)
    stores = []
    for piece in range(PIECES):
        part = pl.ds(piece * share, share)
        stores.append(pltpu.make_async_copy(q2.at[part], new_tracers.at[part], store_sem.at[piece]))

    forcing_copies = ext_copies(forcing, forcing_ext, 1)
    for copy in forcing_copies:
        copy.start()
    for store in stores:
        store.start()
    forcing_ext[0, pl.ds(HALO, rows), :] = forcing[...]
    for copy in forcing_copies:
        copy.wait_recv()
    basis = [join([forcing_ext[0], forcing_ext[1], forcing_ext[2]]) * operator_ext[5]]
    for step in range(ITERS):
        others = neighbours(basis[-1])
        basis.append(sum(operator_ext[n] * others[n] for n in range(4)))
    basis = [vector[HALO:top, :cols] for vector in basis]
    own_diagonal = operator_ext[4, pl.ds(HALO, rows), pl.ds(0, cols)]
    scaled = [own_diagonal * vector for vector in basis[:ITERS]]
    gram_y[0] = jnp.zeros_like(gram_y[0])
    for n in range(2 * ITERS):
        product = scaled[n // 2] * basis[(n + 1) // 2]
        gram_y[0, pl.ds(n, 1), :] = jnp.sum(product, axis=0, keepdims=True)

    def spread(buffer, count, place, axis):
        copies = []
        for step in range(1, count):
            copies.append(
                pltpu.make_async_remote_copy(
                    src_ref=buffer.at[0],
                    dst_ref=buffer.at[step],
                    send_sem=sum_send.at[axis, step],
                    recv_sem=sum_recv.at[axis, step],
                    device_id=place(step),
                    device_id_type=MESH,
                )
            )
        for copy in copies:
            copy.start()
        for copy in copies:
            copy.wait_recv()
        return copies

    y_copies = spread(gram_y, gy, lambda step: device(0, step), 0)
    gram_x[0] = jnp.sum(gram_y[...], axis=0)
    x_copies = spread(gram_x, gx, lambda step: device(step, 0), 1)
    total = jnp.sum(jnp.sum(gram_x[...], axis=0), axis=1, keepdims=True)
    moment = [total[n : n + 1, :] for n in range(2 * ITERS)]

    def inner(left, right):
        terms = [
            a * b * moment[i + j]
            for i, a in enumerate(left) for j, b in enumerate(right)
        ]
        return functools.reduce(lambda x, y: x + y, terms)

    def applied(poly):
        grown = poly + [jnp.zeros_like(poly[0])]
        return [grown[0]] + [grown[n] + grown[n - 1] for n in range(1, len(grown))]

    one = jnp.ones_like(moment[0])
    precond, direction, answer = [one], [one], []
    rz_now = inner(precond, precond)
    for step in range(ITERS):
        image = applied(direction)
        alpha = rz_now / inner(direction, image)
        answer = [
            (answer[n] if n < len(answer) else 0.0) + alpha * direction[n]
            for n in range(len(direction))
        ]
        if step + 1 < ITERS:
            precond = [
                (precond[n] if n < len(precond) else 0.0) - alpha * image[n]
                for n in range(len(image))
            ]
            rz_next = inner(precond, precond)
            beta = rz_next / rz_now
            direction = [
                precond[n] + (beta * direction[n] if n < len(direction) else 0.0)
                for n in range(len(precond))
            ]
            rz_now = rz_next
    pressure[...] = answer[0] * basis[0] + answer[1] * basis[1] + answer[2] * basis[2]

    for copy in level_copies + first_copies + second_copies + forcing_copies + y_copies + x_copies:
        copy.wait_send()
    for store in stores:
        store.wait()


def on_device(gx, gy, tracers, east_flow, north_flow, levels):
    pair, kl, rows, cols = tracers.shape
    planes = pair * kl
    ext = rows + 2 * HALO
    f32 = jnp.float32
    any_space = pl.BlockSpec(memory_space=pl.ANY)
    plane = (kl, rows, cols)
    packed_rows = planes + kl
    new_tracers, pressure = pl.pallas_call(
        functools.partial(fused, gx, gy),
        out_shape=(
            jax.ShapeDtypeStruct((planes, rows, cols), f32),
            jax.ShapeDtypeStruct((rows, cols), f32),
        ),
        in_specs=[any_space] * 4,
        out_specs=(any_space, pl.BlockSpec(memory_space=pltpu.VMEM)),
        scratch_shapes=[
            pltpu.VMEM((planes, ext, cols), f32),
            pltpu.VMEM((planes, ext, cols), f32),
            pltpu.VMEM((planes, rows, cols), f32),
            pltpu.VMEM(plane, jnp.bfloat16),
            pltpu.VMEM(plane, jnp.bfloat16),
            pltpu.VMEM((kl, HALO + rows, cols), f32),
            pltpu.VMEM((rows, cols), jnp.int32),
            pltpu.VMEM((3, ext, cols), jnp.int32),
            pltpu.VMEM(plane, f32),
            pltpu.VMEM(plane, f32),
            pltpu.VMEM(plane, f32),
            pltpu.VMEM(plane, f32),
            pltpu.VMEM(plane, f32),
            pltpu.VMEM((5, rows, cols), f32),
            pltpu.VMEM((6, ext, 2 * cols), f32),
            pltpu.VMEM((2, packed_rows, cols), f32),
            pltpu.VMEM((2, packed_rows, cols), f32),
            pltpu.VMEM((2, packed_rows, cols), f32),
            pltpu.VMEM((2, packed_rows, cols), f32),
            pltpu.VMEM((2, rows, cols), f32),
            pltpu.VMEM((2, 2, rows, cols), f32),
            pltpu.VMEM((rows, cols), f32),
            pltpu.VMEM((rows, cols), f32),
            pltpu.VMEM((3, ext, cols), f32),
            pltpu.VMEM((gy, 8, cols), f32),
            pltpu.VMEM((gx, 8, cols), f32),
            pltpu.SemaphoreType.DMA((3 + PIECES,)),
            pltpu.SemaphoreType.DMA((PIECES,)),
            pltpu.SemaphoreType.DMA((2, 8)),
            pltpu.SemaphoreType.DMA((2, 8)),
            pltpu.SemaphoreType.DMA((2, 4)),
            pltpu.SemaphoreType.DMA((2, 4)),
            pltpu.SemaphoreType.DMA((2, max(gx, gy))),
            pltpu.SemaphoreType.DMA((2, max(gx, gy))),
        ],
        compiler_params=pltpu.CompilerParams(
            collective_id=0, has_side_effects=True, vmem_limit_bytes=48 * 1024 * 1024
        ),
    )(tracers.reshape(planes, rows, cols), east_flow, north_flow, levels)
    return new_tracers.reshape(tracers.shape), pressure


def solution(mesh):
    placed = (P(None, None, "gx", "gy"), P(None, "gx", "gy"), P(None, "gx", "gy"), P("gx", "gy"))
    return jax.shard_map(
        functools.partial(on_device, mesh.shape["gx"], mesh.shape["gy"]),
        mesh=mesh,
        in_specs=placed,
        out_specs=(P(None, None, "gx", "gy"), P("gx", "gy")),
        check_vma=False,
    )
```

time: 411 us -> 47.6 us (0.12)
  blocking collectives: 198 us -> 0 us
  starting transfers between devices: 60 us -> 0 us
  waiting for transfers between devices: 54.8 us -> 0 us
  other arithmetic: 49.2 us -> 0 us
  Pallas kernels: 0 us -> 40.2 us
  local copies, waits for them, and re-layouts: 39 us -> 6.46 us
  between operations: 7.98 us -> 0.65 us
    psum x5 -> x0, blocking collectives: 198 us -> none  [the longest x3 121 us: square_sum(): return lax.psum(jnp.sum(residual * precond), ('gx', 'gy'))]
    ppermute x25 -> x0, waiting for transfers between devices: 41.7 us -> none  [the longest x13 21.1 us: with_halo(): lax.ppermute(lax.slice_in_dim(block, block.shape[dim] - width, None, axis...]
    pallas_call x0 -> x1, Pallas kernels: none -> 40.2 us  [on_device(): pl.pallas_call(functools.partial(fused, gx, gy), out_shape=(jax.ShapeDtyp...]
    ppermute x25 -> x0, starting transfers between devices: 39.6 us -> none  [the longest x12 34 us: with_halo(): lax.ppermute(lax.slice_in_dim(block, 0, width, axis=dim), axis, backward)]
    all_to_all x6 -> x0, starting transfers between devices: 20.4 us -> none  [the longest x1 3.75 us: on_device(): lax.all_to_all(solved, 'gy', split_axis=1, concat_axis=0, tiled=True)]
    slice x19 -> x0, local copies, waits for them, and re-layouts: 15.6 us -> none  [the longest x9 10.2 us: with_halo(): lax.slice_in_dim(block, block.shape[dim] - width, None, axis=dim)]
    sub x4 -> x0, other arithmetic: 14.7 us -> none  [the longest x2 9.79 us: flux_step(): jnp.maximum(north_face, 0.0) * here_y]
    all_to_all x6 -> x0, waiting for transfers between devices: 13.1 us -> none  [the longest x1 4.07 us: on_device(): lax.all_to_all(forcing, 'gy', split_axis=0, concat_axis=1, tiled=True)]
  transfers between devices with their start and end apart: 31 -> 0, of which waited for: 11 -> 0; matrix products, arithmetic and copies ran while one was open for 12% -> 0% of each run, Pallas kernels for 0% -> 0%
where the time goes in v1:
time: 47.6 us; the launch traced here: 47.3 us
  Pallas kernels  40.2 us (84%)
  local copies, waits for them, and re-layouts  6.46 us (14%)
  between operations  0.65 us (1%)
    pallas_call x1, Pallas kernels, on_device(): pl.pallas_call(functools.partial(fused, gx, gy), out_shape=(jax.ShapeDtyp...  40.2 us
    unnamed x10, local copies, waits for them, and re-layouts  6.46 us

profile of v1, /device:TPU:0, one launch (start us, length us, event | category | flops | bytes accessed | tf_op | source)
XLA Modules:
  0.0 47.3 jit_solution(13160417899325099169)
XLA Ops:
  0.6 0.0 copy-start
  0.6 1.6 %copy-done = f32[2,16,128,128]{3,2,1,0:T(8,128)S(1)} copy-done((f32[2,16,128,128]{3,2,1,0:T(8,128)S(1)}, f32[2,16,128,128]{3,2,1,0:T(8,128)}, u32[]{:S(2)}) %copy-start) | copy-done | bytes 2097176
  2.2 0.0 copy-start.1
  2.2 1.0 %copy-done.1 = bf16[16,128,128]{2,1,0:T(8,128)(2,1)S(1)} copy-done((bf16[16,128,128]{2,1,0:T(8,128)(2,1)S(1)}, bf16[16,128,128]{2,1,0:T(8,128)(2,1)}, u32[]{:S(2)}) %copy-start.1) | copy-done | bytes 524312
  3.3 0.0 copy-start.2
  3.3 1.0 %copy-done.2 = bf16[16,128,128]{2,1,0:T(8,128)(2,1)S(1)} copy-done((bf16[16,128,128]{2,1,0:T(8,128)(2,1)S(1)}, bf16[16,128,128]{2,1,0:T(8,128)(2,1)}, u32[]{:S(2)}) %copy-start.2) | copy-done | bytes 524312
  4.3 0.0 copy-start.3
  4.3 0.8 %copy-done.3 = s32[128,128]{1,0:T(8,128)S(1)} copy-done((s32[128,128]{1,0:T(8,128)S(1)}, s32[128,128]{1,0:T(8,128)}, u32[]{:S(2)}) %copy-start.3) | copy-done | bytes 65560
  5.1 40.2 %shard_map.59 = (f32[32,128,128]{2,1,0:T(8,128)S(1)}, f32[128,128]{1,0:T(8,128)S(1)}) custom-call(f32[32,128,128]{2,1,0:T(8,128)S(1)} %bitcast.2, bf16[16,128,128]{2,1,0:T(8,128)(2,1)S(1)} %copy-done.1, bf16[16,128,128]{2,1,0:T(8,128)(2,1)S(1)} %copy-done.2, s32[128,128]{1,0:T(8,128)S(1)} %copy-done.3), custom_call_target="tpu_custom_call" | custom-call | tf_op jit(solution)/shard_map/pallas_call | solution.py:361
  45.3 1.3 %copy.8 = f32[2,16,128,128]{3,2,1,0:T(8,128)} copy(f32[2,16,128,128]{3,2,1,0:T(8,128)S(1)} %bitcast.3) | data formatting | bytes 4194304
  46.6 0.6 %copy.9 = f32[128,128]{1,0:T(8,128)} copy(f32[128,128]{1,0:T(8,128)S(1)} %get-tuple-element.9) | data formatting | bytes 131072
Async XLA Ops:
  0.6 1.6 %copy-start = (f32[2,16,128,128]{3,2,1,0:T(8,128)S(1)}, f32[2,16,128,128]{3,2,1,0:T(8,128)}, u32[]{:S(2)}) copy-start(f32[2,16,128,128]{3,2,1,0:T(8,128)} %param.4) | copy-start | bytes 6291460
  2.2 1.0 %copy-start.1 = (bf16[16,128,128]{2,1,0:T(8,128)(2,1)S(1)}, bf16[16,128,128]{2,1,0:T(8,128)(2,1)}, u32[]{:S(2)}) copy-start(bf16[16,128,128]{2,1,0:T(8,128)(2,1)} %east_flow.1) | copy-start | bytes 1572868
  3.3 1.0 %copy-start.2 = (bf16[16,128,128]{2,1,0:T(8,128)(2,1)S(1)}, bf16[16,128,128]{2,1,0:T(8,128)(2,1)}, u32[]{:S(2)}) copy-start(bf16[16,128,128]{2,1,0:T(8,128)(2,1)} %north_flow.1) | copy-start | bytes 1572868
  4.3 0.8 %copy-start.3 = (s32[128,128]{1,0:T(8,128)S(1)}, s32[128,128]{1,0:T(8,128)}, u32[]{:S(2)}) copy-start(s32[128,128]{1,0:T(8,128)} %levels.1) | copy-start | bytes 196612

commit v2 on v1

v2 whole, which is shorter than its diff:
```python
import functools

import jax
import jax.numpy as jnp
from jax import lax
from jax.experimental import pallas as pl
from jax.experimental.pallas import tpu as pltpu
from jax.sharding import PartitionSpec as P

MESH = pl.DeviceIdType.MESH
ITERS = 3
KAPPA = 0.08
ALPHA = 0.05
HALO = 8
PAD = 16
PIECES = 4


def fused(
    gx, gy,
    tracers, east_flow, north_flow, levels,
    new_tracers, pressure,
    q0, q1, q2, east_raw, north_raw, east_pad, north_pad, level_block, level_ext,
    coef_c, coef_e, coef_w, coef_n, coef_s, reach, side_reach, operator_ext,
    flow_out, flow_in, row_out, row_in, flow_side, q_side, flow_join, east_join, q_join, q_swap,
    forcing_ext, gram_y, gram_x,
    load_sem, store_sem, ext_send, ext_recv, row_send, row_recv,
    sum_send, sum_recv,
):
    planes, rows, cols = tracers.shape
    kl = planes // 2
    top = HALO + rows
    ext = rows + 2 * HALO
    mx = lax.axis_index("gx")
    my = lax.axis_index("gy")
    own = pl.ds(HALO, rows)

    def device(dx, dy):
        return {"gx": lax.rem(mx + dx + gx, gx), "gy": lax.rem(my + dy + gy, gy)}

    loads = [
        pltpu.make_async_copy(levels, level_block, load_sem.at[0]),
        pltpu.make_async_copy(east_flow, east_raw, load_sem.at[1]),
        pltpu.make_async_copy(north_flow, north_raw, load_sem.at[2]),
    ]
    share = planes // PIECES
    for piece in range(PIECES):
        loads.append(
            pltpu.make_async_copy(
                tracers.at[pl.ds(piece * share, share)],
                q0.at[pl.ds(piece * share, share), pl.ds(PAD, rows)],
                load_sem.at[3 + piece],
            )
        )
    for load in loads:
        load.start()

    partners = [(dx, 0) for dx in range(1, gx)] + [(0, dy) for dy in range(1, gy)]
    partners += [(1, 1), (1, -1), (-1, 1), (-1, -1)]
    barrier = pltpu.get_barrier_semaphore()
    for dx, dy in partners:
        pl.semaphore_signal(barrier, inc=1, device_id=device(dx, dy), device_id_type=MESH)

    has_north = my < gy - 1
    has_south = my > 0

    class Exchange:
        def __init__(self, buffer, which, rim, zonal=True):
            last, first, whole = pl.ds(rows, rim), pl.ds(rim, rim), pl.ds(rim, rows)
            low, high = pl.ds(0, rim), pl.ds(rim + rows, rim)
            plan = [
                (0, 1, whole, 2, whole), (0, -1, whole, 1, whole),
                (1, 1, last, 2, low), (-1, 1, first, 2, high),
                (1, -1, last, 1, low), (-1, -1, first, 1, high),
            ]
            if zonal:
                plan += [(1, 0, last, 0, low), (-1, 0, first, 0, high)]
            self.copies = [
                (
                    dy,
                    pltpu.make_async_remote_copy(
                        src_ref=buffer.at[0, source],
                        dst_ref=buffer.at[slot, place],
                        send_sem=ext_send.at[which, n],
                        recv_sem=ext_recv.at[which, n],
                        device_id=device(dx, dy),
                        device_id_type=MESH,
                    ),
                )
                for n, (dx, dy, source, slot, place) in enumerate(plan)
            ]

        def each(self, outward, action):
            for dy, copy in self.copies:
                if dy == 0:
                    action(copy)
                else:
                    pl.when(has_north if (dy > 0) == outward else has_south)(
                        functools.partial(action, copy)
                    )

        def start(self):
            self.each(True, lambda copy: copy.start())

        def wait_recv(self):
            self.each(False, lambda copy: copy.wait_recv())

        def wait_send(self):
            self.each(True, lambda copy: copy.wait_send())

    def row_copies(source, place, which):
        return [
            pltpu.make_async_remote_copy(
                src_ref=source.at[n],
                dst_ref=place.at[n],
                send_sem=row_send.at[which, n],
                recv_sem=row_recv.at[which, n],
                device_id=device(1 - 2 * n, 0),
                device_id_type=MESH,
            )
            for n in range(2)
        ]

    def lanes(count):
        return lax.broadcasted_iota(jnp.int32, (count, cols), 1)

    def rows_out(source, target, base, count):
        for i in range(count):
            target[0, pl.ds(base + 2 * i, 2), :] = source[i, pl.ds(PAD + rows - 2, 2), :]
            target[1, pl.ds(base + 2 * i, 2), :] = source[i, pl.ds(PAD, 2), :]

    def rows_in(source, target, base, count):
        for i in range(count):
            target[i, pl.ds(PAD - 2, 2), :] = source[0, pl.ds(base + 2 * i, 2), :]
            target[i, pl.ds(PAD + rows, 2), :] = source[1, pl.ds(base + 2 * i, 2), :]

    span = 32
    group = lanes(span) >> 2

    def put_side(target, r, pieces):
        place = pl.ds(HALO + r, span)
        total = target[0, place, :]
        for index, value in pieces:
            total = jnp.where(group == index, pltpu.roll(value, 4 * index + 2, 1), total)
        target[0, place, :] = total

    loads[0].wait()
    level_ext[0, pl.ds(PAD, rows), :] = level_block[...].astype(jnp.float32).astype(jnp.bfloat16)
    flow_side[0] = jnp.zeros_like(flow_side[0])
    q_side[0] = jnp.zeros_like(q_side[0])
    loads[1].wait()
    loads[2].wait()

    def take_flow(k, carry):
        for r in range(0, rows, span):
            east = east_raw[k, pl.ds(r, span), :].astype(jnp.float32)
            north = north_raw[k, pl.ds(r, span), :].astype(jnp.float32)
            east_pad[k, pl.ds(PAD + r, span), :] = east
            north_pad[k, pl.ds(PAD + r, span), :] = north
            put_side(flow_side, r, [(k, east), (kl + k, north)])
        return carry

    lax.fori_loop(0, kl, take_flow, 0)
    rows_out(east_pad, flow_out, 0, kl)
    rows_out(north_pad, flow_out, 2 * kl, kl)
    pl.semaphore_wait(barrier, len(partners))
    level_copies = Exchange(level_ext, 0, PAD)
    flow_copies = Exchange(flow_side, 1, HALO, zonal=False)
    q_copies = Exchange(q_side, 2, HALO, zonal=False)
    forcing_copies = Exchange(forcing_ext, 3, HALO)
    flow_rows = row_copies(flow_out, flow_in, 0)
    q_rows = row_copies(row_out, row_in, 1)
    level_copies.start()
    flow_copies.start()
    for copy in flow_rows:
        copy.start()

    for load in loads[3:]:
        load.wait()
    bunch = 4

    def pack(g, carry):
        for r in range(0, rows, span):
            pieces = []
            for j in range(bunch):
                i = g * bunch + j
                pieces.append((i, q0[i, pl.ds(PAD + r, span), :]))
            put_side(q_side, r, pieces)
        return carry

    lax.fori_loop(0, planes // bunch, pack, 0)
    q_copies.start()
    rows_out(q0, row_out, 0, planes)
    for copy in q_rows:
        copy.start()

    level_copies.wait_recv()
    lane_ext = lanes(ext)
    north_lanes = jnp.where(has_north, cols, 0)
    south_lanes = jnp.where(has_south, cols, 0)

    def known(north, south, lane):
        return (
            jnp.where(lane < north_lanes, north, 0.0),
            jnp.where(lane < south_lanes, south, 0.0),
        )

    def join(parts):
        north, south = known(parts[1], parts[2], lane_ext)
        return jnp.concatenate(
            [parts[0], jnp.where(lane_ext < cols // 2, north, south)], axis=1
        )

    def neighbours(value):
        return (
            pltpu.roll(value, ext - 1, 0), pltpu.roll(value, 1, 0),
            pltpu.roll(value, 2 * cols - 1, 1), pltpu.roll(value, 1, 1),
        )

    trim = PAD - HALO
    depth = join(
        [level_ext[n].astype(jnp.float32)[trim : trim + ext] for n in range(3)]
    ) / kl
    sides = [jnp.minimum(depth, other) for other in neighbours(depth)]
    diagonal = ALPHA * depth + (depth == 0.0).astype(jnp.float32)
    diagonal = diagonal + sides[0] + sides[1] + sides[2] + sides[3]
    inverse = 1.0 / diagonal
    lane = lanes(rows)
    corner = lane & 3
    for n, side in enumerate(sides + [depth]):
        if n < 4:
            operator_ext[n] = -side * inverse
        scaled_side = side * kl
        reach[n] = scaled_side[:, :cols]
        edge = scaled_side[HALO:top, cols:]
        side_reach[n] = jnp.where(corner == 1, edge[:, cols - 1 : cols], edge[:, :1])
    operator_ext[4] = diagonal
    operator_ext[5] = inverse

    def merge(side):
        north, south = known(side[1], side[2], lane_ext)
        return jnp.where((lane_ext & 3) >= 2, north, south)

    def coefficients(level, limit, east, west, north, south):
        def gate(n, value):
            return jnp.where(level < limit(n), value, 0.0)

        def out_of(face):
            return jnp.maximum(face, 0.0) + KAPPA

        def back(face):
            return KAPPA - jnp.minimum(face, 0.0)

        lost = gate(0, out_of(east)) + gate(1, back(west)) + gate(2, out_of(north)) + gate(3, back(south))
        return (
            gate(4, 1.0 - lost), gate(0, back(east)), gate(1, out_of(west)),
            gate(2, back(north)), gate(3, out_of(south)),
        )

    flow_copies.wait_recv()
    for copy in flow_rows:
        copy.wait_recv()
    rows_in(flow_in, east_pad, 0, kl)
    rows_in(flow_in, north_pad, 2 * kl, kl)
    flow_join[...] = merge(flow_side)
    wide = 24
    lane_wide = lanes(wide)

    def prepare(k, carry):
        level = k.astype(jnp.float32)
        for e in range(0, ext, wide):
            part = pl.ds(e, wide)
            east = east_pad[k, pl.ds(HALO + e, wide), :]
            west = east_pad[k, pl.ds(HALO + e - 1, wide), :]
            north = north_pad[k, pl.ds(HALO + e, wide), :]
            halo = pltpu.roll(flow_join[part, :], cols // 2 - 1 - 4 * k, 1)
            south = jnp.where(lane_wide == 0, halo, pltpu.roll(north, 1, 1))
            result = coefficients(level, lambda n: reach[n, part, :], east, west, north, south)
            for ref, value in zip((coef_c, coef_e, coef_w, coef_n, coef_s), result):
                ref[k, part, :] = value
        return carry

    lax.fori_loop(0, kl, prepare, 0)

    half = cols // 2
    joined = flow_join[...]
    turned = pltpu.roll(joined, half, 1)
    east_join[...] = jnp.where(lane_ext < half, joined, turned)
    north_side = jnp.where(lane_ext < half, turned, joined)[HALO:top]
    own_flow = flow_side[0, own, :]
    own_north = jnp.where(lane < half, pltpu.roll(own_flow, half, 1), own_flow)
    south_side = jnp.where(corner == 2, pltpu.roll(own_north, 1, 1), pltpu.roll(north_side, 1, 1))
    side_level = ((lane & (half - 1)) >> 2).astype(jnp.float32)
    side_coef = coefficients(
        side_level, lambda n: side_reach[n],
        east_join[own, :], east_join[pl.ds(HALO - 1, rows), :], north_side, south_side,
    )
    q_copies.wait_recv()
    q_join[...] = merge(q_side)
    here = q_join[own, :]
    own_side = q_side[0, own, :]
    north = jnp.where(corner == 1, pltpu.roll(own_side, cols - 1, 1), pltpu.roll(here, cols - 1, 1))
    south = jnp.where(corner == 2, pltpu.roll(own_side, 1, 1), pltpu.roll(here, 1, 1))
    moved = (
        side_coef[0] * here
        + side_coef[1] * q_join[pl.ds(HALO + 1, rows), :]
        + side_coef[2] * q_join[pl.ds(HALO - 1, rows), :]
        + side_coef[3] * north
        + side_coef[4] * south
    )

    def swap(value, place):
        return jnp.where((place & 3) == 1, pltpu.roll(value, cols - 1, 1), pltpu.roll(value, 1, 1))

    q_swap[0] = swap(q_join[...], lane_ext)
    q_swap[1, own, :] = swap(moved, lane)

    for copy in q_rows:
        copy.wait_recv()
    rows_in(row_in, q0, 0, planes)

    def advance(q, which, i, k, e, count, lane_here):
        part = pl.ds(e, count)
        here = q[i, pl.ds(HALO + e, count), :]
        halo = pltpu.roll(q_swap[which, part, :], cols - 2 - 4 * i, 1)
        north = jnp.where(lane_here == cols - 1, halo, pltpu.roll(here, cols - 1, 1))
        south = jnp.where(lane_here == 0, halo, pltpu.roll(here, 1, 1))
        return (
            coef_c[k, part, :] * here
            + coef_e[k, part, :] * q[i, pl.ds(HALO + e + 1, count), :]
            + coef_w[k, part, :] * q[i, pl.ds(HALO + e - 1, count), :]
            + coef_n[k, part, :] * north
            + coef_s[k, part, :] * south
        )

    def first_step(k, carry):
        for e in range(0, ext, wide):
            for tracer in range(2):
                i = tracer * kl + k
                q1[i, pl.ds(HALO + e, wide), :] = advance(q0, 0, i, k, e, wide, lane_wide)
        return carry

    lax.fori_loop(0, kl, first_step, 0)
    forcing_ext[0, own, :] = jnp.zeros((rows, cols), jnp.float32)
    lane_span = lanes(span)

    def second_step(k, carry):
        for r in range(0, rows, span):
            heat = advance(q1, 1, k, k, HALO + r, span, lane_span)
            salt = advance(q1, 1, kl + k, k, HALO + r, span, lane_span)
            q2[k, pl.ds(r, span), :] = heat
            q2[kl + k, pl.ds(r, span), :] = salt
            forcing_ext[0, pl.ds(HALO + r, span), :] += 0.25 * (heat - 0.8 * salt)
        return carry

    lax.fori_loop(0, kl, second_step, 0)
    forcing_copies.start()
    stores = []
    for piece in range(PIECES):
        part = pl.ds(piece * share, share)
        stores.append(pltpu.make_async_copy(q2.at[part], new_tracers.at[part], store_sem.at[piece]))
    for store in stores:
        store.start()

    forcing_copies.wait_recv()
    basis = [join([forcing_ext[0], forcing_ext[1], forcing_ext[2]]) * operator_ext[5]]
    for step in range(ITERS):
        others = neighbours(basis[-1])
        basis.append(sum(operator_ext[n] * others[n] for n in range(4)))
    basis = [vector[HALO:top, :cols] for vector in basis]
    own_diagonal = operator_ext[4, pl.ds(HALO, rows), pl.ds(0, cols)]
    scaled = [own_diagonal * vector for vector in basis[:ITERS]]
    gram_y[0] = jnp.zeros_like(gram_y[0])
    for n in range(2 * ITERS):
        product = scaled[n // 2] * basis[(n + 1) // 2]
        gram_y[0, pl.ds(n, 1), :] = jnp.sum(product, axis=0, keepdims=True)

    def spread(buffer, count, place, axis):
        copies = []
        for step in range(1, count):
            copies.append(
                pltpu.make_async_remote_copy(
                    src_ref=buffer.at[0],
                    dst_ref=buffer.at[step],
                    send_sem=sum_send.at[axis, step],
                    recv_sem=sum_recv.at[axis, step],
                    device_id=place(step),
                    device_id_type=MESH,
                )
            )
        for copy in copies:
            copy.start()
        for copy in copies:
            copy.wait_recv()
        return copies

    y_copies = spread(gram_y, gy, lambda step: device(0, step), 0)
    gram_x[0] = jnp.sum(gram_y[...], axis=0)
    x_copies = spread(gram_x, gx, lambda step: device(step, 0), 1)
    total = jnp.sum(jnp.sum(gram_x[...], axis=0), axis=1, keepdims=True)
    moment = [total[n : n + 1, :] for n in range(2 * ITERS)]

    def inner(left, right):
        terms = [
            a * b * moment[i + j]
            for i, a in enumerate(left) for j, b in enumerate(right)
        ]
        return functools.reduce(lambda x, y: x + y, terms)

    def applied(poly):
        grown = poly + [jnp.zeros_like(poly[0])]
        return [grown[0]] + [grown[n] + grown[n - 1] for n in range(1, len(grown))]

    one = jnp.ones_like(moment[0])
    precond, direction, answer = [one], [one], []
    rz_now = inner(precond, precond)
    for step in range(ITERS):
        image = applied(direction)
        alpha = rz_now / inner(direction, image)
        answer = [
            (answer[n] if n < len(answer) else 0.0) + alpha * direction[n]
            for n in range(len(direction))
        ]
        if step + 1 < ITERS:
            precond = [
                (precond[n] if n < len(precond) else 0.0) - alpha * image[n]
                for n in range(len(image))
            ]
            rz_next = inner(precond, precond)
            beta = rz_next / rz_now
            direction = [
                precond[n] + (beta * direction[n] if n < len(direction) else 0.0)
                for n in range(len(precond))
            ]
            rz_now = rz_next
    pressure[...] = answer[0] * basis[0] + answer[1] * basis[1] + answer[2] * basis[2]

    for exchange in (level_copies, flow_copies, q_copies, forcing_copies):
        exchange.wait_send()
    for copy in flow_rows + q_rows + y_copies + x_copies:
        copy.wait_send()
    for store in stores:
        store.wait()


def on_device(gx, gy, tracers, east_flow, north_flow, levels):
    pair, kl, rows, cols = tracers.shape
    planes = pair * kl
    ext = rows + 2 * HALO
    pad = rows + 2 * PAD
    f32 = jnp.float32
    in_hbm = pl.BlockSpec(memory_space=pltpu.HBM)
    plane = (kl, rows, cols)
    wide_plane = (kl, ext, cols)
    new_tracers, pressure = pl.pallas_call(
        functools.partial(fused, gx, gy),
        out_shape=(
            jax.ShapeDtypeStruct((planes, rows, cols), f32),
            jax.ShapeDtypeStruct((rows, cols), f32),
        ),
        in_specs=[in_hbm] * 4,
        out_specs=(in_hbm, pl.BlockSpec(memory_space=pltpu.VMEM)),
        scratch_shapes=[
            pltpu.VMEM((planes, pad, cols), f32),
            pltpu.VMEM((planes, pad, cols), f32),
            pltpu.VMEM((planes, rows, cols), f32),
            pltpu.VMEM(plane, jnp.bfloat16),
            pltpu.VMEM(plane, jnp.bfloat16),
            pltpu.VMEM((kl, pad, cols), f32),
            pltpu.VMEM((kl, pad, cols), f32),
            pltpu.VMEM((rows, cols), jnp.int32),
            pltpu.VMEM((3, pad, cols), jnp.bfloat16),
            pltpu.VMEM(wide_plane, f32),
            pltpu.VMEM(wide_plane, f32),
            pltpu.VMEM(wide_plane, f32),
            pltpu.VMEM(wide_plane, f32),
            pltpu.VMEM(wide_plane, f32),
            pltpu.VMEM((5, ext, cols), f32),
            pltpu.VMEM((5, rows, cols), f32),
            pltpu.VMEM((6, ext, 2 * cols), f32),
            pltpu.VMEM((2, 4 * kl, cols), f32),
            pltpu.VMEM((2, 4 * kl, cols), f32),
            pltpu.VMEM((2, 2 * planes, cols), f32),
            pltpu.VMEM((2, 2 * planes, cols), f32),
            pltpu.VMEM((3, ext, cols), f32),
            pltpu.VMEM((3, ext, cols), f32),
            pltpu.VMEM((ext, cols), f32),
            pltpu.VMEM((ext, cols), f32),
            pltpu.VMEM((ext, cols), f32),
            pltpu.VMEM((2, ext, cols), f32),
            pltpu.VMEM((3, ext, cols), f32),
            pltpu.VMEM((gy, 8, cols), f32),
            pltpu.VMEM((gx, 8, cols), f32),
            pltpu.SemaphoreType.DMA((3 + PIECES,)),
            pltpu.SemaphoreType.DMA((PIECES,)),
            pltpu.SemaphoreType.DMA((4, 8)),
            pltpu.SemaphoreType.DMA((4, 8)),
            pltpu.SemaphoreType.DMA((2, 2)),
            pltpu.SemaphoreType.DMA((2, 2)),
            pltpu.SemaphoreType.DMA((2, max(gx, gy))),
            pltpu.SemaphoreType.DMA((2, max(gx, gy))),
        ],
        compiler_params=pltpu.CompilerParams(
            collective_id=0, has_side_effects=True, vmem_limit_bytes=60 * 1024 * 1024
        ),
    )(tracers.reshape(planes, rows, cols), east_flow, north_flow, levels)
    return new_tracers.reshape(tracers.shape), pressure


def solution(mesh):
    placed = (P(None, None, "gx", "gy"), P(None, "gx", "gy"), P(None, "gx", "gy"), P("gx", "gy"))
    return jax.shard_map(
        functools.partial(on_device, mesh.shape["gx"], mesh.shape["gy"]),
        mesh=mesh,
        in_specs=placed,
        out_specs=(P(None, None, "gx", "gy"), P("gx", "gy")),
        check_vma=False,
    )
```

time: 47.6 us -> 37.2 us (0.78)
  Pallas kernels: 40.2 us -> 32.6 us
  local copies, waits for them, and re-layouts: 6.46 us -> 3.8 us
    pallas_call x1, Pallas kernels: 40.2 us -> 32.6 us  [on_device(): pl.pallas_call(functools.partial(fused, gx, gy), out_shape=(jax.ShapeDtyp...]
    unnamed x10 -> x4, local copies, waits for them, and re-layouts: 6.46 us -> 3.8 us
where the time goes in v2:
time: 37.2 us; the launch traced here: 37 us
  Pallas kernels  32.6 us (88%)
  local copies, waits for them, and re-layouts  3.8 us (10%)
  between operations  0.65 us (2%)
    pallas_call x1, Pallas kernels, on_device(): pl.pallas_call(functools.partial(fused, gx, gy), out_shape=(jax.ShapeDtyp...  32.6 us
    unnamed x4, local copies, waits for them, and re-layouts  3.8 us

profile of v2, /device:TPU:0, one launch (start us, length us, event | category | flops | bytes accessed | tf_op | source)
XLA Modules:
  0.0 37.0 jit_solution(2707838964819621137)
XLA Ops:
  0.6 32.6 %shard_map.59 = (f32[32,128,128]{2,1,0:T(8,128)}, f32[128,128]{1,0:T(8,128)}) custom-call(f32[32,128,128]{2,1,0:T(8,128)} %bitcast.2, bf16[16,128,128]{2,1,0:T(8,128)(2,1)} %east_flow.1, bf16[16,128,128]{2,1,0:T(8,128)(2,1)} %north_flow.1, s32[128,128]{1,0:T(8,128)} %levels.1), custom_call_target="tpu_custom_call" | custom-call | tf_op jit(solution)/shard_map/pallas_call | solution.py:455
  33.2 0.0 copy-start
  33.2 3.2 %copy.8 = f32[2,16,128,128]{3,2,1,0:T(8,128)} copy(f32[2,16,128,128]{3,2,1,0:T(8,128)} %bitcast.3) | data formatting | bytes 4194304
  36.4 0.0 copy-done
  36.4 0.6 %copy.9 = f32[128,128]{1,0:T(8,128)} copy(f32[128,128]{1,0:T(8,128)S(1)} %copy-done) | data formatting | bytes 131072
Async XLA Ops:
  33.2 3.2 %copy-start = (f32[128,128]{1,0:T(8,128)S(1)}, f32[128,128]{1,0:T(8,128)}, u32[]{:S(2)}) copy-start(f32[128,128]{1,0:T(8,128)} %get-tuple-element.9) | copy-start | bytes 196612

commit v3 on v2

--- a/solution.py
+++ b/solution.py
@@ -19,12 +19,12 @@
 def fused(
     gx, gy,
     tracers, east_flow, north_flow, levels,
-    new_tracers, pressure,
-    q0, q1, q2, east_raw, north_raw, east_pad, north_pad, level_block, level_ext,
+    q2, pressure,
+    q0, q1, east_raw, north_raw, east_pad, north_pad, level_block, level_ext,
     coef_c, coef_e, coef_w, coef_n, coef_s, reach, side_reach, operator_ext,
     flow_out, flow_in, row_out, row_in, flow_side, q_side, flow_join, east_join, q_join, q_swap,
-    forcing_ext, gram_y, gram_x,
-    load_sem, store_sem, ext_send, ext_recv, row_send, row_recv,
+    forcing_ext, gram_tile, gram,
+    load_sem, ext_send, ext_recv, row_send, row_recv,
     sum_send, sum_recv,
 ):
     planes, rows, cols = tracers.shape
@@ -55,10 +55,9 @@
     for load in loads:
         load.start()
 
-    partners = [(dx, 0) for dx in range(1, gx)] + [(0, dy) for dy in range(1, gy)]
-    partners += [(1, 1), (1, -1), (-1, 1), (-1, -1)]
+    others = [(dx, dy) for dx in range(gx) for dy in range(gy) if (dx, dy) != (0, 0)]
     barrier = pltpu.get_barrier_semaphore()
-    for dx, dy in partners:
+    for dx, dy in others:
         pl.semaphore_signal(barrier, inc=1, device_id=device(dx, dy), device_id_type=MESH)
 
     has_north = my < gy - 1
@@ -134,7 +133,7 @@
             target[i, pl.ds(PAD - 2, 2), :] = source[0, pl.ds(base + 2 * i, 2), :]
             target[i, pl.ds(PAD + rows, 2), :] = source[1, pl.ds(base + 2 * i, 2), :]
 
-    span = 32
+    span = 64
     group = lanes(span) >> 2
 
     def put_side(target, r, pieces):
@@ -144,10 +143,18 @@
             total = jnp.where(group == index, pltpu.roll(value, 4 * index + 2, 1), total)
         target[0, place, :] = total
 
+    level_copies = Exchange(level_ext, 0, PAD)
+    flow_copies = Exchange(flow_side, 1, HALO, zonal=False)
+    q_copies = Exchange(q_side, 2, HALO, zonal=False)
+    forcing_copies = Exchange(forcing_ext, 3, HALO)
+    flow_rows = row_copies(flow_out, flow_in, 0)
+    q_rows = row_copies(row_out, row_in, 1)
+    flow_side[0] = jnp.zeros_like(flow_side[0])
+    q_side[0] = jnp.zeros_like(q_side[0])
     loads[0].wait()
     level_ext[0, pl.ds(PAD, rows), :] = level_block[...].astype(jnp.float32).astype(jnp.bfloat16)
-    flow_side[0] = jnp.zeros_like(flow_side[0])
-    q_side[0] = jnp.zeros_like(q_side[0])
+    pl.semaphore_wait(barrier, len(others))
+    level_copies.start()
     loads[1].wait()
     loads[2].wait()
 
@@ -163,14 +170,6 @@
     lax.fori_loop(0, kl, take_flow, 0)
     rows_out(east_pad, flow_out, 0, kl)
     rows_out(north_pad, flow_out, 2 * kl, kl)
-    pl.semaphore_wait(barrier, len(partners))
-    level_copies = Exchange(level_ext, 0, PAD)
-    flow_copies = Exchange(flow_side, 1, HALO, zonal=False)
-    q_copies = Exchange(q_side, 2, HALO, zonal=False)
-    forcing_copies = Exchange(forcing_ext, 3, HALO)
-    flow_rows = row_copies(flow_out, flow_in, 0)
-    q_rows = row_copies(row_out, row_in, 1)
-    level_copies.start()
     flow_copies.start()
     for copy in flow_rows:
         copy.start()
@@ -263,7 +262,7 @@
     rows_in(flow_in, east_pad, 0, kl)
     rows_in(flow_in, north_pad, 2 * kl, kl)
     flow_join[...] = merge(flow_side)
-    wide = 24
+    wide = 48
     lane_wide = lanes(wide)
 
     def prepare(k, carry):
@@ -355,49 +354,44 @@
 
     lax.fori_loop(0, kl, second_step, 0)
     forcing_copies.start()
-    stores = []
-    for piece in range(PIECES):
-        part = pl.ds(piece * share, share)
-        stores.append(pltpu.make_async_copy(q2.at[part], new_tracers.at[part], store_sem.at[piece]))
-    for store in stores:
-        store.start()
 
     forcing_copies.wait_recv()
     basis = [join([forcing_ext[0], forcing_ext[1], forcing_ext[2]]) * operator_ext[5]]
     for step in range(ITERS):
-        others = neighbours(basis[-1])
-        basis.append(sum(operator_ext[n] * others[n] for n in range(4)))
+        around = neighbours(basis[-1])
+        basis.append(sum(operator_ext[n] * around[n] for n in range(4)))
     basis = [vector[HALO:top, :cols] for vector in basis]
     own_diagonal = operator_ext[4, pl.ds(HALO, rows), pl.ds(0, cols)]
     scaled = [own_diagonal * vector for vector in basis[:ITERS]]
-    gram_y[0] = jnp.zeros_like(gram_y[0])
+    gram_tile[...] = jnp.zeros_like(gram_tile)
     for n in range(2 * ITERS):
         product = scaled[n // 2] * basis[(n + 1) // 2]
-        gram_y[0, pl.ds(n, 1), :] = jnp.sum(product, axis=0, keepdims=True)
-
-    def spread(buffer, count, place, axis):
-        copies = []
-        for step in range(1, count):
-            copies.append(
-                pltpu.make_async_remote_copy(
-                    src_ref=buffer.at[0],
-                    dst_ref=buffer.at[step],
-                    send_sem=sum_send.at[axis, step],
-                    recv_sem=sum_recv.at[axis, step],
-                    device_id=place(step),
-                    device_id_type=MESH,
-                )
-            )
-        for copy in copies:
-            copy.start()
-        for copy in copies:
-            copy.wait_recv()
-        return copies
-
-    y_copies = spread(gram_y, gy, lambda step: device(0, step), 0)
-    gram_x[0] = jnp.sum(gram_y[...], axis=0)
-    x_copies = spread(gram_x, gx, lambda step: device(step, 0), 1)
-    total = jnp.sum(jnp.sum(gram_x[...], axis=0), axis=1, keepdims=True)
+        gram_tile[pl.ds(n, 1), :] = jnp.sum(product, axis=0, keepdims=True)
+
+    mine = (lanes(8) >> 4) == lax.broadcasted_iota(jnp.int32, (8, cols), 0)
+    tile = gram_tile[...]
+    for fold in (cols // 2, cols // 4, cols // 8):
+        tile = tile + pltpu.roll(tile, fold, 1)
+    gram[0] = jnp.sum(jnp.where(mine, tile, 0.0), axis=0, keepdims=True)
+    sum_copies = [
+        pltpu.make_async_remote_copy(
+            src_ref=gram.at[0],
+            dst_ref=gram.at[dx * gy + dy],
+            send_sem=sum_send.at[dx * gy + dy],
+            recv_sem=sum_recv.at[dx * gy + dy],
+            device_id=device(dx, dy),
+            device_id_type=MESH,
+        )
+        for dx, dy in others
+    ]
+    for copy in sum_copies:
+        copy.start()
+    for copy in sum_copies:
+        copy.wait_recv()
+    row = gram[0]
+    for n in range(1, gx * gy):
+        row = row + gram[n]
+    total = jnp.sum(jnp.where(mine, row, 0.0), axis=1, keepdims=True)
     moment = [total[n : n + 1, :] for n in range(2 * ITERS)]
 
     def inner(left, right):
@@ -437,10 +431,8 @@
 
     for exchange in (level_copies, flow_copies, q_copies, forcing_copies):
         exchange.wait_send()
-    for copy in flow_rows + q_rows + y_copies + x_copies:
+    for copy in flow_rows + q_rows + sum_copies:
         copy.wait_send()
-    for store in stores:
-        store.wait()
 
 
 def on_device(gx, gy, tracers, east_flow, north_flow, levels):
@@ -455,15 +447,14 @@
     new_tracers, pressure = pl.pallas_call(
         functools.partial(fused, gx, gy),
         out_shape=(
-            jax.ShapeDtypeStruct((planes, rows, cols), f32),
-            jax.ShapeDtypeStruct((rows, cols), f32),
+            pltpu.VMEM((planes, rows, cols), f32),
+            pltpu.VMEM((rows, cols), f32),
         ),
         in_specs=[in_hbm] * 4,
-        out_specs=(in_hbm, pl.BlockSpec(memory_space=pltpu.VMEM)),
+        out_specs=(pl.BlockSpec(memory_space=pltpu.VMEM),) * 2,
         scratch_shapes=[
             pltpu.VMEM((planes, pad, cols), f32),
             pltpu.VMEM((planes, pad, cols), f32),
-            pltpu.VMEM((planes, rows, cols), f32),
             pltpu.VMEM(plane, jnp.bfloat16),
             pltpu.VMEM(plane, jnp.bfloat16),
             pltpu.VMEM((kl, pad, cols), f32),
@@ -489,16 +480,15 @@
             pltpu.VMEM((ext, cols), f32),
             pltpu.VMEM((2, ext, cols), f32),
             pltpu.VMEM((3, ext, cols), f32),
-            pltpu.VMEM((gy, 8, cols), f32),
-            pltpu.VMEM((gx, 8, cols), f32),
+            pltpu.VMEM((8, cols), f32),
+            pltpu.VMEM((gx * gy, 1, cols), f32),
             pltpu.SemaphoreType.DMA((3 + PIECES,)),
-            pltpu.SemaphoreType.DMA((PIECES,)),
             pltpu.SemaphoreType.DMA((4, 8)),
             pltpu.SemaphoreType.DMA((4, 8)),
             pltpu.SemaphoreType.DMA((2, 2)),
             pltpu.SemaphoreType.DMA((2, 2)),
-            pltpu.SemaphoreType.DMA((2, max(gx, gy))),
-            pltpu.SemaphoreType.DMA((2, max(gx, gy))),
+            pltpu.SemaphoreType.DMA((gx * gy,)),
+            pltpu.SemaphoreType.DMA((gx * gy,)),
         ],
         compiler_params=pltpu.CompilerParams(
             collective_id=0, has_side_effects=True, vmem_limit_bytes=60 * 1024 * 1024

time: 37.2 us -> 33.8 us (0.909)
  local copies, waits for them, and re-layouts: 3.8 us -> 1.95 us
  Pallas kernels: 32.6 us -> 31 us
    unnamed x4 -> x2, local copies, waits for them, and re-layouts: 3.8 us -> 1.95 us
    pallas_call x1, Pallas kernels: 32.6 us -> 31 us  [on_device(): pl.pallas_call(functools.partial(fused, gx, gy), out_shape=(pltpu.VMEM((p...]
where the time goes in v3:
time: 33.8 us; the launch traced here: 33.6 us
  Pallas kernels  31 us (92%)
  local copies, waits for them, and re-layouts  1.95 us (6%)
  between operations  0.64 us (2%)
    pallas_call x1, Pallas kernels, on_device(): pl.pallas_call(functools.partial(fused, gx, gy), out_shape=(pltpu.VMEM((p...  31 us
    unnamed x2, local copies, waits for them, and re-layouts  1.95 us

profile of v3, /device:TPU:0, one launch (start us, length us, event | category | flops | bytes accessed | tf_op | source)
XLA Modules:
  0.0 33.6 jit_solution(3440118060694821859)
XLA Ops:
  0.6 31.0 %shard_map.59 = (f32[32,128,128]{2,1,0:T(8,128)S(1)}, f32[128,128]{1,0:T(8,128)S(1)}) custom-call(f32[32,128,128]{2,1,0:T(8,128)} %bitcast.3, bf16[16,128,128]{2,1,0:T(8,128)(2,1)} %east_flow.1, bf16[16,128,128]{2,1,0:T(8,128)(2,1)} %north_flow.1, s32[128,128]{1,0:T(8,128)} %levels.1), custom_call_target="tpu_custom_call" | custom-call | tf_op jit(solution)/shard_map/pallas_call | solution.py:447
  31.7 1.3 %copy.8 = f32[2,16,128,128]{3,2,1,0:T(8,128)} copy(f32[2,16,128,128]{3,2,1,0:T(8,128)S(1)} %bitcast.2) | data formatting | bytes 4194304
  33.0 0.6 %copy.9 = f32[128,128]{1,0:T(8,128)} copy(f32[128,128]{1,0:T(8,128)S(1)} %get-tuple-element.7) | data formatting | bytes 131072

commit v4 on v3

--- a/solution.py
+++ b/solution.py
@@ -20,8 +20,8 @@
     gx, gy,
     tracers, east_flow, north_flow, levels,
     q2, pressure,
-    q0, q1, east_raw, north_raw, east_pad, north_pad, level_block, level_ext,
-    coef_c, coef_e, coef_w, coef_n, coef_s, reach, side_reach, operator_ext,
+    q0, q1_a, q1_b, east_raw, north_raw, east_pad, north_pad, level_block, level_ext,
+    coef_a, coef_b, reach, side_reach, operator_ext,
     flow_out, flow_in, row_out, row_in, flow_side, q_side, flow_join, east_join, q_join, q_swap,
     forcing_ext, gram_tile, gram,
     load_sem, ext_send, ext_recv, row_send, row_recv,
@@ -133,7 +133,7 @@
             target[i, pl.ds(PAD - 2, 2), :] = source[0, pl.ds(base + 2 * i, 2), :]
             target[i, pl.ds(PAD + rows, 2), :] = source[1, pl.ds(base + 2 * i, 2), :]
 
-    span = 64
+    span = 32
     group = lanes(span) >> 2
 
     def put_side(target, r, pieces):
@@ -262,25 +262,6 @@
     rows_in(flow_in, east_pad, 0, kl)
     rows_in(flow_in, north_pad, 2 * kl, kl)
     flow_join[...] = merge(flow_side)
-    wide = 48
-    lane_wide = lanes(wide)
-
-    def prepare(k, carry):
-        level = k.astype(jnp.float32)
-        for e in range(0, ext, wide):
-            part = pl.ds(e, wide)
-            east = east_pad[k, pl.ds(HALO + e, wide), :]
-            west = east_pad[k, pl.ds(HALO + e - 1, wide), :]
-            north = north_pad[k, pl.ds(HALO + e, wide), :]
-            halo = pltpu.roll(flow_join[part, :], cols // 2 - 1 - 4 * k, 1)
-            south = jnp.where(lane_wide == 0, halo, pltpu.roll(north, 1, 1))
-            result = coefficients(level, lambda n: reach[n, part, :], east, west, north, south)
-            for ref, value in zip((coef_c, coef_e, coef_w, coef_n, coef_s), result):
-                ref[k, part, :] = value
-        return carry
-
-    lax.fori_loop(0, kl, prepare, 0)
-
     half = cols // 2
     joined = flow_join[...]
     turned = pltpu.roll(joined, half, 1)
@@ -318,41 +299,77 @@
         copy.wait_recv()
     rows_in(row_in, q0, 0, planes)
 
-    def advance(q, which, i, k, e, count, lane_here):
-        part = pl.ds(e, count)
-        here = q[i, pl.ds(HALO + e, count), :]
-        halo = pltpu.roll(q_swap[which, part, :], cols - 2 - 4 * i, 1)
+    wide = 24
+    lane_wide = lanes(wide)
+    lane_span = lanes(span)
+    forcing_ext[0, own, :] = jnp.zeros((rows, cols), jnp.float32)
+
+    def advance(here, east, west, halo, coef, lane_here):
         north = jnp.where(lane_here == cols - 1, halo, pltpu.roll(here, cols - 1, 1))
         south = jnp.where(lane_here == 0, halo, pltpu.roll(here, 1, 1))
         return (
-            coef_c[k, part, :] * here
-            + coef_e[k, part, :] * q[i, pl.ds(HALO + e + 1, count), :]
-            + coef_w[k, part, :] * q[i, pl.ds(HALO + e - 1, count), :]
-            + coef_n[k, part, :] * north
-            + coef_s[k, part, :] * south
-        )
-
-    def first_step(k, carry):
-        for e in range(0, ext, wide):
-            for tracer in range(2):
-                i = tracer * kl + k
-                q1[i, pl.ds(HALO + e, wide), :] = advance(q0, 0, i, k, e, wide, lane_wide)
+            coef[0] * here + coef[1] * east + coef[2] * west
+            + coef[3] * north + coef[4] * south
+        )
+
+    def first_step(k, coef_ref, q_ref, e):
+        part = pl.ds(e, wide)
+        level = lax.convert_element_type(k, jnp.float32)
+        east = east_pad[k, pl.ds(HALO + e, wide), :]
+        west = east_pad[k, pl.ds(HALO + e - 1, wide), :]
+        north = north_pad[k, pl.ds(HALO + e, wide), :]
+        halo = pltpu.roll(flow_join[part, :], cols // 2 - 1 - 4 * k, 1)
+        south = jnp.where(lane_wide == 0, halo, pltpu.roll(north, 1, 1))
+        coef = coefficients(level, lambda n: reach[n, part, :], east, west, north, south)
+        for n in range(5):
+            coef_ref[n, part, :] = coef[n]
+        for tracer in range(2):
+            i = tracer * kl + k
+            q_ref[tracer, pl.ds(HALO + e, wide), :] = advance(
+                q0[i, pl.ds(HALO + e, wide), :],
+                q0[i, pl.ds(HALO + e + 1, wide), :],
+                q0[i, pl.ds(HALO + e - 1, wide), :],
+                pltpu.roll(q_swap[0, part, :], cols - 2 - 4 * i, 1),
+                coef, lane_wide,
+            )
+
+    def second_step(k, coef_ref, q_ref, r):
+        part = pl.ds(HALO + r, span)
+        coef = [coef_ref[n, part, :] for n in range(5)]
+        result = []
+        for tracer in range(2):
+            i = tracer * kl + k
+            value = advance(
+                q_ref[tracer, pl.ds(PAD + r, span), :],
+                q_ref[tracer, pl.ds(PAD + r + 1, span), :],
+                q_ref[tracer, pl.ds(PAD + r - 1, span), :],
+                pltpu.roll(q_swap[1, part, :], cols - 2 - 4 * i, 1),
+                coef, lane_span,
+            )
+            q2[i, pl.ds(r, span), :] = value
+            result.append(value)
+        forcing_ext[0, part, :] += 0.25 * (result[0] - 0.8 * result[1])
+
+    def beside(first, second):
+        ahead = [functools.partial(first_step, *first, e) for e in range(0, ext, wide)] if first else []
+        behind = [functools.partial(second_step, *second, r) for r in range(0, rows, span)] if second else []
+        for n in range(max(len(ahead), len(behind))):
+            for chunks in (ahead, behind):
+                if n < len(chunks):
+                    chunks[n]()
+
+    slot_a, slot_b = (coef_a, q1_a), (coef_b, q1_b)
+    beside((0, *slot_a), None)
+
+    def two_levels(j, carry):
+        k = 2 * j
+        beside((k + 1, *slot_b), (k, *slot_a))
+        beside((k + 2, *slot_a), (k + 1, *slot_b))
         return carry
 
-    lax.fori_loop(0, kl, first_step, 0)
-    forcing_ext[0, own, :] = jnp.zeros((rows, cols), jnp.float32)
-    lane_span = lanes(span)
-
-    def second_step(k, carry):
-        for r in range(0, rows, span):
-            heat = advance(q1, 1, k, k, HALO + r, span, lane_span)
-            salt = advance(q1, 1, kl + k, k, HALO + r, span, lane_span)
-            q2[k, pl.ds(r, span), :] = heat
-            q2[kl + k, pl.ds(r, span), :] = salt
-            forcing_ext[0, pl.ds(HALO + r, span), :] += 0.25 * (heat - 0.8 * salt)
-        return carry
-
-    lax.fori_loop(0, kl, second_step, 0)
+    lax.fori_loop(0, kl // 2 - 1, two_levels, 0)
+    beside((kl - 1, *slot_b), (kl - 2, *slot_a))
+    beside(None, (kl - 1, *slot_b))
     forcing_copies.start()
 
     forcing_copies.wait_recv()
@@ -443,7 +460,6 @@
     f32 = jnp.float32
     in_hbm = pl.BlockSpec(memory_space=pltpu.HBM)
     plane = (kl, rows, cols)
-    wide_plane = (kl, ext, cols)
     new_tracers, pressure = pl.pallas_call(
         functools.partial(fused, gx, gy),
         out_shape=(
@@ -454,18 +470,16 @@
         out_specs=(pl.BlockSpec(memory_space=pltpu.VMEM),) * 2,
         scratch_shapes=[
             pltpu.VMEM((planes, pad, cols), f32),
-            pltpu.VMEM((planes, pad, cols), f32),
+            pltpu.VMEM((2, pad, cols), f32),
+            pltpu.VMEM((2, pad, cols), f32),
             pltpu.VMEM(plane, jnp.bfloat16),
             pltpu.VMEM(plane, jnp.bfloat16),
             pltpu.VMEM((kl, pad, cols), f32),
             pltpu.VMEM((kl, pad, cols), f32),
             pltpu.VMEM((rows, cols), jnp.int32),
             pltpu.VMEM((3, pad, cols), jnp.bfloat16),
-            pltpu.VMEM(wide_plane, f32),
-            pltpu.VMEM(wide_plane, f32),
-            pltpu.VMEM(wide_plane, f32),
-            pltpu.VMEM(wide_plane, f32),
-            pltpu.VMEM(wide_plane, f32),
+            pltpu.VMEM((5, ext, cols), f32),
+            pltpu.VMEM((5, ext, cols), f32),
             pltpu.VMEM((5, ext, cols), f32),
             pltpu.VMEM((5, rows, cols), f32),
             pltpu.VMEM((6, ext, 2 * cols), f32),

time: 33.8 us -> 31.2 us (0.923)
  Pallas kernels: 31 us -> 28.5 us
    pallas_call x1, Pallas kernels: 31 us -> 28.5 us  [on_device(): pl.pallas_call(functools.partial(fused, gx, gy), out_shape=(pltpu.VMEM((p...]
where the time goes in v4:
time: 31.2 us; the launch traced here: 31 us
  Pallas kernels  28.5 us (91%)
  local copies, waits for them, and re-layouts  1.95 us (6%)
  between operations  0.64 us (2%)
    pallas_call x1, Pallas kernels, on_device(): pl.pallas_call(functools.partial(fused, gx, gy), out_shape=(pltpu.VMEM((p...  28.5 us
    unnamed x2, local copies, waits for them, and re-layouts  1.95 us

profile of v4, /device:TPU:0, one launch (start us, length us, event | category | flops | bytes accessed | tf_op | source)
XLA Modules:
  0.0 31.0 jit_solution(14272799518840386495)
XLA Ops:
  0.6 28.5 %shard_map.59 = (f32[32,128,128]{2,1,0:T(8,128)S(1)}, f32[128,128]{1,0:T(8,128)S(1)}) custom-call(f32[32,128,128]{2,1,0:T(8,128)} %bitcast.3, bf16[16,128,128]{2,1,0:T(8,128)(2,1)} %east_flow.1, bf16[16,128,128]{2,1,0:T(8,128)(2,1)} %north_flow.1, s32[128,128]{1,0:T(8,128)} %levels.1), custom_call_target="tpu_custom_call" | custom-call | tf_op jit(solution)/shard_map/pallas_call | solution.py:463
  29.1 1.3 %copy.8 = f32[2,16,128,128]{3,2,1,0:T(8,128)} copy(f32[2,16,128,128]{3,2,1,0:T(8,128)S(1)} %bitcast.2) | data formatting | bytes 4194304
  30.4 0.6 %copy.9 = f32[128,128]{1,0:T(8,128)} copy(f32[128,128]{1,0:T(8,128)S(1)} %get-tuple-element.7) | data formatting | bytes 131072

commit v5 on v4

--- a/solution.py
+++ b/solution.py
@@ -123,15 +123,21 @@
     def lanes(count):
         return lax.broadcasted_iota(jnp.int32, (count, cols), 1)
 
+    def row_of(ref, row):
+        count, height, _ = ref.shape
+        return ref.reshape(count * height, cols), pl.ds(row, count, stride=height)
+
     def rows_out(source, target, base, count):
-        for i in range(count):
-            target[0, pl.ds(base + 2 * i, 2), :] = source[i, pl.ds(PAD + rows - 2, 2), :]
-            target[1, pl.ds(base + 2 * i, 2), :] = source[i, pl.ds(PAD, 2), :]
+        for n, first in ((0, PAD + rows - 2), (1, PAD)):
+            for j in range(2):
+                flat, place = row_of(source, first + j)
+                target[n, pl.ds(base + j * count, count), :] = flat[place, :]
 
     def rows_in(source, target, base, count):
-        for i in range(count):
-            target[i, pl.ds(PAD - 2, 2), :] = source[0, pl.ds(base + 2 * i, 2), :]
-            target[i, pl.ds(PAD + rows, 2), :] = source[1, pl.ds(base + 2 * i, 2), :]
+        for n, first in ((0, PAD - 2), (1, PAD + rows)):
+            for j in range(2):
+                flat, place = row_of(target, first + j)
+                flat[place, :] = source[n, pl.ds(base + j * count, count), :]
 
     span = 32
     group = lanes(span) >> 2
@@ -158,16 +164,20 @@
     loads[1].wait()
     loads[2].wait()
 
-    def take_flow(k, carry):
+    def take_flow(g, carry):
         for r in range(0, rows, span):
-            east = east_raw[k, pl.ds(r, span), :].astype(jnp.float32)
-            north = north_raw[k, pl.ds(r, span), :].astype(jnp.float32)
-            east_pad[k, pl.ds(PAD + r, span), :] = east
-            north_pad[k, pl.ds(PAD + r, span), :] = north
-            put_side(flow_side, r, [(k, east), (kl + k, north)])
+            pieces = []
+            for j in range(2):
+                k = 2 * g + j
+                east = east_raw[k, pl.ds(r, span), :].astype(jnp.float32)
+                north = north_raw[k, pl.ds(r, span), :].astype(jnp.float32)
+                east_pad[k, pl.ds(PAD + r, span), :] = east
+                north_pad[k, pl.ds(PAD + r, span), :] = north
+                pieces += [(k, east), (kl + k, north)]
+            put_side(flow_side, r, pieces)
         return carry
 
-    lax.fori_loop(0, kl, take_flow, 0)
+    lax.fori_loop(0, kl // 2, take_flow, 0)
     rows_out(east_pad, flow_out, 0, kl)
     rows_out(north_pad, flow_out, 2 * kl, kl)
     flow_copies.start()
@@ -316,13 +326,28 @@
         part = pl.ds(e, wide)
         level = lax.convert_element_type(k, jnp.float32)
         east = east_pad[k, pl.ds(HALO + e, wide), :]
-        west = east_pad[k, pl.ds(HALO + e - 1, wide), :]
         north = north_pad[k, pl.ds(HALO + e, wide), :]
         halo = pltpu.roll(flow_join[part, :], cols // 2 - 1 - 4 * k, 1)
         south = jnp.where(lane_wide == 0, halo, pltpu.roll(north, 1, 1))
-        coef = coefficients(level, lambda n: reach[n, part, :], east, west, north, south)
-        for n in range(5):
-            coef_ref[n, part, :] = coef[n]
+
+        def gated(n, face):
+            is_open = level < reach[n, part, :]
+            face = jnp.where(is_open, face, 0.0)
+            out = jnp.maximum(face, 0.0) + jnp.where(is_open, KAPPA, 0.0)
+            return out, out - face
+
+        east_out, east_back = gated(0, east)
+        coef_ref[1, pl.ds(HALO + e, wide), :] = east_back
+        coef_ref[2, pl.ds(HALO + e, wide), :] = east_out
+        north_out, north_back = gated(2, north)
+        south_out, south_back = gated(3, south)
+        west_back = coef_ref[1, pl.ds(HALO + e - 1, wide), :]
+        west_out = coef_ref[2, pl.ds(HALO + e - 1, wide), :]
+        lost = east_out + west_back + north_out + south_back
+        centre = jnp.where(level < reach[4, part, :], 1.0 - lost, 0.0)
+        coef = (centre, east_back, west_out, north_back, south_out)
+        for n in (0, 3, 4):
+            coef_ref[n, pl.ds(HALO + e, wide), :] = coef[n]
         for tracer in range(2):
             i = tracer * kl + k
             q_ref[tracer, pl.ds(HALO + e, wide), :] = advance(
@@ -335,7 +360,7 @@
 
     def second_step(k, coef_ref, q_ref, r):
         part = pl.ds(HALO + r, span)
-        coef = [coef_ref[n, part, :] for n in range(5)]
+        coef = [coef_ref[n, pl.ds(PAD + r - (n == 2), span), :] for n in range(5)]
         result = []
         for tracer in range(2):
             i = tracer * kl + k
@@ -478,8 +503,8 @@
             pltpu.VMEM((kl, pad, cols), f32),
             pltpu.VMEM((rows, cols), jnp.int32),
             pltpu.VMEM((3, pad, cols), jnp.bfloat16),
-            pltpu.VMEM((5, ext, cols), f32),
-            pltpu.VMEM((5, ext, cols), f32),
+            pltpu.VMEM((5, pad, cols), f32),
+            pltpu.VMEM((5, pad, cols), f32),
             pltpu.VMEM((5, ext, cols), f32),
             pltpu.VMEM((5, rows, cols), f32),
             pltpu.VMEM((6, ext, 2 * cols), f32),

time: 31.2 us -> 30.7 us (0.984)
  Pallas kernels: 28.5 us -> 28 us
    pallas_call x1, Pallas kernels: 28.5 us -> 28 us  [on_device(): pl.pallas_call(functools.partial(fused, gx, gy), out_shape=(pltpu.VMEM((p...]
where the time goes in v5:
time: 30.7 us; the launch traced here: 30.5 us
  Pallas kernels  28 us (91%)
  local copies, waits for them, and re-layouts  1.95 us (6%)
  between operations  0.64 us (2%)
    pallas_call x1, Pallas kernels, on_device(): pl.pallas_call(functools.partial(fused, gx, gy), out_shape=(pltpu.VMEM((p...  28 us
    unnamed x2, local copies, waits for them, and re-layouts  1.95 us

profile of v5, /device:TPU:0, one launch (start us, length us, event | category | flops | bytes accessed | tf_op | source)
XLA Modules:
  0.0 30.5 jit_solution(4607378951103967372)
XLA Ops:
  0.6 28.0 %shard_map.59 = (f32[32,128,128]{2,1,0:T(8,128)S(1)}, f32[128,128]{1,0:T(8,128)S(1)}) custom-call(f32[32,128,128]{2,1,0:T(8,128)} %bitcast.3, bf16[16,128,128]{2,1,0:T(8,128)(2,1)} %east_flow.1, bf16[16,128,128]{2,1,0:T(8,128)(2,1)} %north_flow.1, s32[128,128]{1,0:T(8,128)} %levels.1), custom_call_target="tpu_custom_call" | custom-call | tf_op jit(solution)/shard_map/pallas_call | solution.py:488
  28.6 1.3 %copy.8 = f32[2,16,128,128]{3,2,1,0:T(8,128)} copy(f32[2,16,128,128]{3,2,1,0:T(8,128)S(1)} %bitcast.2) | data formatting | bytes 4194304
  29.9 0.6 %copy.9 = f32[128,128]{1,0:T(8,128)} copy(f32[128,128]{1,0:T(8,128)S(1)} %get-tuple-element.7) | data formatting | bytes 131072

commit v6 on v5

--- a/solution.py
+++ b/solution.py
@@ -52,7 +52,7 @@
                 load_sem.at[3 + piece],
             )
         )
-    for load in loads:
+    for load in loads[:3]:
         load.start()
 
     others = [(dx, dy) for dx in range(gx) for dy in range(gy) if (dx, dy) != (0, 0)]
@@ -163,6 +163,8 @@
     level_copies.start()
     loads[1].wait()
     loads[2].wait()
+    for load in loads[3:]:
+        load.start()
 
     def take_flow(g, carry):
         for r in range(0, rows, span):
@@ -475,6 +477,18 @@
         exchange.wait_send()
     for copy in flow_rows + q_rows + sum_copies:
         copy.wait_send()
+
+
+def hand_over(tracers, pressure, new_tracers, new_pressure, sem):
+    share = tracers.shape[0] // PIECES
+    copies = [pltpu.make_async_copy(pressure, new_pressure, sem.at[PIECES])]
+    for piece in range(PIECES):
+        part = pl.ds(piece * share, share)
+        copies.append(pltpu.make_async_copy(tracers.at[part], new_tracers.at[part], sem.at[piece]))
+    for copy in copies:
+        copy.start()
+    for copy in copies:
+        copy.wait()
 
 
 def on_device(gx, gy, tracers, east_flow, north_flow, levels):
@@ -533,6 +547,16 @@
             collective_id=0, has_side_effects=True, vmem_limit_bytes=60 * 1024 * 1024
         ),
     )(tracers.reshape(planes, rows, cols), east_flow, north_flow, levels)
+    new_tracers, pressure = pl.pallas_call(
+        hand_over,
+        out_shape=(
+            jax.ShapeDtypeStruct((planes, rows, cols), f32),
+            jax.ShapeDtypeStruct((rows, cols), f32),
+        ),
+        in_specs=[pl.BlockSpec(memory_space=pltpu.VMEM)] * 2,
+        out_specs=(in_hbm, in_hbm),
+        scratch_shapes=[pltpu.SemaphoreType.DMA((PIECES + 1,))],
+    )(new_tracers, pressure)
     return new_tracers.reshape(tracers.shape), pressure
 
 

time: 30.7 us -> 33.7 us (1.098)
  Pallas kernels: 28 us -> 30.9 us
    pallas_call x0 -> x1, Pallas kernels: none -> 2.97 us  [on_device(): pl.pallas_call(hand_over, out_shape=(jax.ShapeDtypeStruct((planes, rows,...]
    unnamed x2 -> x4, local copies, waits for them, and re-layouts: 1.95 us -> 1.94 us
where the time goes in v6:
time: 33.7 us; the launch traced here: 33.5 us
  Pallas kernels  30.9 us (92%)
  local copies, waits for them, and re-layouts  1.94 us (6%)
  between operations  0.65 us (2%)
    pallas_call x1, Pallas kernels, on_device(): pl.pallas_call(functools.partial(fused, gx, gy), out_shape=(pltpu.VMEM((p...  27.9 us
    pallas_call x1, Pallas kernels, on_device(): pl.pallas_call(hand_over, out_shape=(jax.ShapeDtypeStruct((planes, rows,...  2.97 us
    unnamed x4, local copies, waits for them, and re-layouts  1.94 us

profile of v6, /device:TPU:0, one launch (start us, length us, event | category | flops | bytes accessed | tf_op | source)
XLA Modules:
  0.0 33.5 jit_solution(3106424735542010285)
XLA Ops:
  0.6 27.9 %shard_map.59 = (f32[32,128,128]{2,1,0:T(8,128)S(1)}, f32[128,128]{1,0:T(8,128)S(1)}) custom-call(f32[32,128,128]{2,1,0:T(8,128)} %bitcast.2, bf16[16,128,128]{2,1,0:T(8,128)(2,1)} %east_flow.1, bf16[16,128,128]{2,1,0:T(8,128)(2,1)} %north_flow.1, s32[128,128]{1,0:T(8,128)} %levels.1), custom_call_target="tpu_custom_call" | custom-call | tf_op jit(solution)/shard_map/pallas_call | solution.py:502
  28.6 0.0 copy-start
  28.6 1.3 %copy-done = f32[32,128,128]{2,1,0:T(8,128)} copy-done((f32[32,128,128]{2,1,0:T(8,128)}, f32[32,128,128]{2,1,0:T(8,128)S(1)}, u32[]{:S(2)}) %copy-start) | copy-done | bytes 2097176
  29.9 0.0 copy-start.1
  29.9 0.6 %copy-done.1 = f32[128,128]{1,0:T(8,128)} copy-done((f32[128,128]{1,0:T(8,128)}, f32[128,128]{1,0:T(8,128)S(1)}, u32[]{:S(2)}) %copy-start.1) | copy-done | bytes 65560
  30.5 3.0 %shard_map.60 = (f32[32,128,128]{2,1,0:T(8,128)}, f32[128,128]{1,0:T(8,128)}) custom-call(f32[32,128,128]{2,1,0:T(8,128)} %copy-done, f32[128,128]{1,0:T(8,128)} %copy-done.1), custom_call_target="tpu_custom_call" | custom-call | tf_op jit(solution)/shard_map/pallas_call | solution.py:550
Async XLA Ops:
  28.6 1.3 %copy-start = (f32[32,128,128]{2,1,0:T(8,128)}, f32[32,128,128]{2,1,0:T(8,128)S(1)}, u32[]{:S(2)}) copy-start(f32[32,128,128]{2,1,0:T(8,128)S(1)} %get-tuple-element.6.tracers) | copy-start | bytes 6291460
  29.9 0.6 %copy-start.1 = (f32[128,128]{1,0:T(8,128)}, f32[128,128]{1,0:T(8,128)S(1)}, u32[]{:S(2)}) copy-start(f32[128,128]{1,0:T(8,128)S(1)} %get-tuple-element.7.pressure) | copy-start | bytes 196612

commit v7 on v5

--- a/solution.py
+++ b/solution.py
@@ -20,10 +20,10 @@
     gx, gy,
     tracers, east_flow, north_flow, levels,
     q2, pressure,
-    q0, q1_a, q1_b, east_raw, north_raw, east_pad, north_pad, level_block, level_ext,
+    q0, q1_a, q1_b, east_raw, north_raw, east_pad, north_pad, level_block, level_ext, level_rim,
     coef_a, coef_b, reach, side_reach, operator_ext,
     flow_out, flow_in, row_out, row_in, flow_side, q_side, flow_join, east_join, q_join, q_swap,
-    forcing_ext, gram_tile, gram,
+    forcing_ext, forcing_rim, gram_tile, gram,
     load_sem, ext_send, ext_recv, row_send, row_recv,
     sum_send, sum_recv,
 ):
@@ -34,6 +34,7 @@
     mx = lax.axis_index("gx")
     my = lax.axis_index("gy")
     own = pl.ds(HALO, rows)
+    own_first = pl.ds(HALO, HALO)
 
     def device(dx, dy):
         return {"gx": lax.rem(mx + dx + gx, gx), "gy": lax.rem(my + dy + gy, gy)}
@@ -64,16 +65,15 @@
     has_south = my > 0
 
     class Exchange:
-        def __init__(self, buffer, which, rim, zonal=True):
-            last, first, whole = pl.ds(rows, rim), pl.ds(rim, rim), pl.ds(rim, rows)
-            low, high = pl.ds(0, rim), pl.ds(rim + rows, rim)
+        def __init__(self, buffer, which, zonal=None):
+            count, rim = buffer.shape[1] - 2 * HALO, HALO
+            last, first, whole = pl.ds(count, rim), pl.ds(rim, rim), pl.ds(rim, count)
+            low, high = pl.ds(0, rim), pl.ds(rim + count, rim)
             plan = [
                 (0, 1, whole, 2, whole), (0, -1, whole, 1, whole),
                 (1, 1, last, 2, low), (-1, 1, first, 2, high),
                 (1, -1, last, 1, low), (-1, -1, first, 1, high),
             ]
-            if zonal:
-                plan += [(1, 0, last, 0, low), (-1, 0, first, 0, high)]
             self.copies = [
                 (
                     dy,
@@ -88,6 +88,19 @@
                 )
                 for n, (dx, dy, source, slot, place) in enumerate(plan)
             ]
+            if zonal is not None:
+                for n, (dx, source, place) in enumerate(
+                    [(1, pl.ds(rows, HALO), pl.ds(0, HALO)), (-1, own_first, pl.ds(top, HALO))]
+                ):
+                    copy = pltpu.make_async_remote_copy(
+                        src_ref=zonal.at[source],
+                        dst_ref=zonal.at[place],
+                        send_sem=ext_send.at[which, len(plan) + n],
+                        recv_sem=ext_recv.at[which, len(plan) + n],
+                        device_id=device(dx, 0),
+                        device_id_type=MESH,
+                    )
+                    self.copies.append((0, copy))
 
         def each(self, outward, action):
             for dy, copy in self.copies:
@@ -149,16 +162,42 @@
             total = jnp.where(group == index, pltpu.roll(value, 4 * index + 2, 1), total)
         target[0, place, :] = total
 
-    level_copies = Exchange(level_ext, 0, PAD)
-    flow_copies = Exchange(flow_side, 1, HALO, zonal=False)
-    q_copies = Exchange(q_side, 2, HALO, zonal=False)
-    forcing_copies = Exchange(forcing_ext, 3, HALO)
+    level_copies = Exchange(level_rim, 0, level_ext)
+    flow_copies = Exchange(flow_side, 1)
+    q_copies = Exchange(q_side, 2)
+    forcing_copies = Exchange(forcing_rim, 3, forcing_ext)
     flow_rows = row_copies(flow_out, flow_in, 0)
     q_rows = row_copies(row_out, row_in, 1)
     flow_side[0] = jnp.zeros_like(flow_side[0])
     q_side[0] = jnp.zeros_like(q_side[0])
+    tall = 2 * HALO
+    folds = rows // tall
+
+    def fold_rim(source, rim):
+        lane_tall = lanes(tall)
+        total = jnp.zeros((tall, cols), jnp.float32)
+        for c in range(folds):
+            value = pltpu.roll(source[pl.ds(HALO + c * tall, tall), :], 8 * c + 4, 1)
+            total = jnp.where(lane_tall >> 3 == c, value, total)
+        rim[0, pl.ds(HALO, tall), :] = total
+
+    def unfold_rim(rim):
+        lane_rim = lanes(2 * tall)
+        north, south = known(rim[1], rim[2], lane_rim)
+        joint = jnp.where((lane_rim & 7) >= 4, north, south)
+
+        def turn(value, c):
+            return pltpu.roll(value, cols - 4 - 8 * c, 1)
+
+        middle = joint[HALO : HALO + tall]
+        parts = [turn(joint[:HALO], folds - 1)]
+        parts += [turn(middle, c) for c in range(folds)]
+        parts.append(turn(joint[HALO + tall :], 0))
+        return jnp.concatenate(parts, axis=0)
+
     loads[0].wait()
-    level_ext[0, pl.ds(PAD, rows), :] = level_block[...].astype(jnp.float32).astype(jnp.bfloat16)
+    level_ext[own, :] = level_block[...].astype(jnp.float32)
+    fold_rim(level_ext, level_rim)
     pl.semaphore_wait(barrier, len(others))
     level_copies.start()
     loads[1].wait()
@@ -214,11 +253,8 @@
             jnp.where(lane < south_lanes, south, 0.0),
         )
 
-    def join(parts):
-        north, south = known(parts[1], parts[2], lane_ext)
-        return jnp.concatenate(
-            [parts[0], jnp.where(lane_ext < cols // 2, north, south)], axis=1
-        )
+    def join(value, rim):
+        return jnp.concatenate([value[...], unfold_rim(rim)], axis=1)
 
     def neighbours(value):
         return (
@@ -226,10 +262,7 @@
             pltpu.roll(value, 2 * cols - 1, 1), pltpu.roll(value, 1, 1),
         )
 
-    trim = PAD - HALO
-    depth = join(
-        [level_ext[n].astype(jnp.float32)[trim : trim + ext] for n in range(3)]
-    ) / kl
+    depth = join(level_ext, level_rim) / kl
     sides = [jnp.minimum(depth, other) for other in neighbours(depth)]
     diagonal = ALPHA * depth + (depth == 0.0).astype(jnp.float32)
     diagonal = diagonal + sides[0] + sides[1] + sides[2] + sides[3]
@@ -312,7 +345,7 @@
     wide = 24
     lane_wide = lanes(wide)
     lane_span = lanes(span)
-    forcing_ext[0, own, :] = jnp.zeros((rows, cols), jnp.float32)
+    forcing_ext[own, :] = jnp.zeros((rows, cols), jnp.float32)
 
     def advance(here, east, west, halo, coef, lane_here):
         north = jnp.where(lane_here == cols - 1, halo, pltpu.roll(here, cols - 1, 1))
@@ -373,7 +406,7 @@
             )
             q2[i, pl.ds(r, span), :] = value
             result.append(value)
-        forcing_ext[0, part, :] += 0.25 * (result[0] - 0.8 * result[1])
+        forcing_ext[part, :] += 0.25 * (result[0] - 0.8 * result[1])
 
     def beside(first, second):
         ahead = [functools.partial(first_step, *first, e) for e in range(0, ext, wide)] if first else []
@@ -395,10 +428,11 @@
     lax.fori_loop(0, kl // 2 - 1, two_levels, 0)
     beside((kl - 1, *slot_b), (kl - 2, *slot_a))
     beside(None, (kl - 1, *slot_b))
+    fold_rim(forcing_ext, forcing_rim)
     forcing_copies.start()
 
     forcing_copies.wait_recv()
-    basis = [join([forcing_ext[0], forcing_ext[1], forcing_ext[2]]) * operator_ext[5]]
+    basis = [join(forcing_ext, forcing_rim) * operator_ext[5]]
     for step in range(ITERS):
         around = neighbours(basis[-1])
         basis.append(sum(operator_ext[n] * around[n] for n in range(4)))
@@ -502,7 +536,8 @@
             pltpu.VMEM((kl, pad, cols), f32),
             pltpu.VMEM((kl, pad, cols), f32),
             pltpu.VMEM((rows, cols), jnp.int32),
-            pltpu.VMEM((3, pad, cols), jnp.bfloat16),
+            pltpu.VMEM((ext, cols), f32),
+            pltpu.VMEM((3, 4 * HALO, cols), f32),
             pltpu.VMEM((5, pad, cols), f32),
             pltpu.VMEM((5, pad, cols), f32),
             pltpu.VMEM((5, ext, cols), f32),
@@ -518,7 +553,8 @@
             pltpu.VMEM((ext, cols), f32),
             pltpu.VMEM((ext, cols), f32),
             pltpu.VMEM((2, ext, cols), f32),
-            pltpu.VMEM((3, ext, cols), f32),
+            pltpu.VMEM((ext, cols), f32),
+            pltpu.VMEM((3, 4 * HALO, cols), f32),
             pltpu.VMEM((8, cols), f32),
             pltpu.VMEM((gx * gy, 1, cols), f32),
             pltpu.SemaphoreType.DMA((3 + PIECES,)),

time: 30.7 us -> 30.8 us (level)
  no operation moved by 1% of the time
where the time goes in v7:
time: 30.8 us; the launch traced here: 30.6 us
  Pallas kernels  28.1 us (91%)
  local copies, waits for them, and re-layouts  1.95 us (6%)
  between operations  0.64 us (2%)
    pallas_call x1, Pallas kernels, on_device(): pl.pallas_call(functools.partial(fused, gx, gy), out_shape=(pltpu.VMEM((p...  28.1 us
    unnamed x2, local copies, waits for them, and re-layouts  1.95 us

profile of v7, /device:TPU:0, one launch (start us, length us, event | category | flops | bytes accessed | tf_op | source)
XLA Modules:
  0.0 30.6 jit_solution(3112655183849423707)
XLA Ops:
  0.6 28.1 %shard_map.59 = (f32[32,128,128]{2,1,0:T(8,128)S(1)}, f32[128,128]{1,0:T(8,128)S(1)}) custom-call(f32[32,128,128]{2,1,0:T(8,128)} %bitcast.3, bf16[16,128,128]{2,1,0:T(8,128)(2,1)} %east_flow.1, bf16[16,128,128]{2,1,0:T(8,128)(2,1)} %north_flow.1, s32[128,128]{1,0:T(8,128)} %levels.1), custom_call_target="tpu_custom_call" | custom-call | tf_op jit(solution)/shard_map/pallas_call | solution.py:522
  28.7 1.3 %copy.8 = f32[2,16,128,128]{3,2,1,0:T(8,128)} copy(f32[2,16,128,128]{3,2,1,0:T(8,128)S(1)} %bitcast.2) | data formatting | bytes 4194304
  30.0 0.6 %copy.9 = f32[128,128]{1,0:T(8,128)} copy(f32[128,128]{1,0:T(8,128)S(1)} %get-tuple-element.7) | data formatting | bytes 131072

commit v8 on v5

--- a/solution.py
+++ b/solution.py
@@ -55,7 +55,9 @@
     for load in loads:
         load.start()
 
-    others = [(dx, dy) for dx in range(gx) for dy in range(gy) if (dx, dy) != (0, 0)]
+    along_x = [(dx, 0) for dx in range(1, gx)]
+    along_y = [(0, dy) for dy in range(1, gy)]
+    others = along_x + along_y + [(1, 1), (1, -1), (-1, 1), (-1, -1)]
     barrier = pltpu.get_barrier_semaphore()
     for dx, dy in others:
         pl.semaphore_signal(barrier, inc=1, device_id=device(dx, dy), device_id_type=MESH)
@@ -396,6 +398,10 @@
     beside((kl - 1, *slot_b), (kl - 2, *slot_a))
     beside(None, (kl - 1, *slot_b))
     forcing_copies.start()
+    for exchange in (level_copies, flow_copies, q_copies):
+        exchange.wait_send()
+    for copy in flow_rows + q_rows:
+        copy.wait_send()
 
     forcing_copies.wait_recv()
     basis = [join([forcing_ext[0], forcing_ext[1], forcing_ext[2]]) * operator_ext[5]]
@@ -415,24 +421,37 @@
     for fold in (cols // 2, cols // 4, cols // 8):
         tile = tile + pltpu.roll(tile, fold, 1)
     gram[0] = jnp.sum(jnp.where(mine, tile, 0.0), axis=0, keepdims=True)
-    sum_copies = [
-        pltpu.make_async_remote_copy(
-            src_ref=gram.at[0],
-            dst_ref=gram.at[dx * gy + dy],
-            send_sem=sum_send.at[dx * gy + dy],
-            recv_sem=sum_recv.at[dx * gy + dy],
-            device_id=device(dx, dy),
-            device_id_type=MESH,
-        )
-        for dx, dy in others
-    ]
-    for copy in sum_copies:
-        copy.start()
-    for copy in sum_copies:
-        copy.wait_recv()
-    row = gram[0]
-    for n in range(1, gx * gy):
-        row = row + gram[n]
+
+    def spread(base, targets):
+        copies = [
+            pltpu.make_async_remote_copy(
+                src_ref=gram.at[base],
+                dst_ref=gram.at[base + dx + dy],
+                send_sem=sum_send.at[base + dx + dy],
+                recv_sem=sum_recv.at[base + dx + dy],
+                device_id=device(dx, dy),
+                device_id_type=MESH,
+            )
+            for dx, dy in targets
+        ]
+        for copy in copies:
+            copy.start()
+        return copies
+
+    def gather(base, copies):
+        for copy in copies:
+            copy.wait_recv()
+        row = gram[base]
+        for n in range(1, len(copies) + 1):
+            row = row + gram[base + n]
+        return row
+
+    y_copies = spread(0, along_y)
+    forcing_copies.wait_send()
+    gram[gy] = gather(0, y_copies)
+    x_copies = spread(gy, along_x)
+    sum_copies = y_copies + x_copies
+    row = gather(gy, x_copies)
     total = jnp.sum(jnp.where(mine, row, 0.0), axis=1, keepdims=True)
     moment = [total[n : n + 1, :] for n in range(2 * ITERS)]
 
@@ -471,9 +490,7 @@
             rz_now = rz_next
     pressure[...] = answer[0] * basis[0] + answer[1] * basis[1] + answer[2] * basis[2]
 
-    for exchange in (level_copies, flow_copies, q_copies, forcing_copies):
-        exchange.wait_send()
-    for copy in flow_rows + q_rows + sum_copies:
+    for copy in sum_copies:
         copy.wait_send()
 
 
@@ -520,14 +537,14 @@
             pltpu.VMEM((2, ext, cols), f32),
             pltpu.VMEM((3, ext, cols), f32),
             pltpu.VMEM((8, cols), f32),
-            pltpu.VMEM((gx * gy, 1, cols), f32),
+            pltpu.VMEM((gx + gy, 1, cols), f32),
             pltpu.SemaphoreType.DMA((3 + PIECES,)),
             pltpu.SemaphoreType.DMA((4, 8)),
             pltpu.SemaphoreType.DMA((4, 8)),
             pltpu.SemaphoreType.DMA((2, 2)),
             pltpu.SemaphoreType.DMA((2, 2)),
-            pltpu.SemaphoreType.DMA((gx * gy,)),
-            pltpu.SemaphoreType.DMA((gx * gy,)),
+            pltpu.SemaphoreType.DMA((gx + gy,)),
+            pltpu.SemaphoreType.DMA((gx + gy,)),
         ],
         compiler_params=pltpu.CompilerParams(
             collective_id=0, has_side_effects=True, vmem_limit_bytes=60 * 1024 * 1024

time: 30.7 us -> 32 us (1.042)
  Pallas kernels: 28 us -> 29.2 us
    pallas_call x1, Pallas kernels: 28 us -> 29.2 us  [on_device(): pl.pallas_call(functools.partial(fused, gx, gy), out_shape=(pltpu.VMEM((p...]
where the time goes in v8:
time: 32 us; the launch traced here: 31.8 us
  Pallas kernels  29.2 us (91%)
  local copies, waits for them, and re-layouts  1.95 us (6%)
  between operations  0.64 us (2%)
    pallas_call x1, Pallas kernels, on_device(): pl.pallas_call(functools.partial(fused, gx, gy), out_shape=(pltpu.VMEM((p...  29.2 us
    unnamed x2, local copies, waits for them, and re-layouts  1.95 us

profile of v8, /device:TPU:0, one launch (start us, length us, event | category | flops | bytes accessed | tf_op | source)
XLA Modules:
  0.0 31.8 jit_solution(1488992075509498637)
XLA Ops:
  0.6 29.2 %shard_map.59 = (f32[32,128,128]{2,1,0:T(8,128)S(1)}, f32[128,128]{1,0:T(8,128)S(1)}) custom-call(f32[32,128,128]{2,1,0:T(8,128)} %bitcast.3, bf16[16,128,128]{2,1,0:T(8,128)(2,1)} %east_flow.1, bf16[16,128,128]{2,1,0:T(8,128)(2,1)} %north_flow.1, s32[128,128]{1,0:T(8,128)} %levels.1), custom_call_target="tpu_custom_call" | custom-call | tf_op jit(solution)/shard_map/pallas_call | solution.py:505
  29.9 1.3 %copy.8 = f32[2,16,128,128]{3,2,1,0:T(8,128)} copy(f32[2,16,128,128]{3,2,1,0:T(8,128)S(1)} %bitcast.2) | data formatting | bytes 4194304
  31.2 0.6 %copy.9 = f32[128,128]{1,0:T(8,128)} copy(f32[128,128]{1,0:T(8,128)S(1)} %get-tuple-element.7) | data formatting | bytes 131072
